TPU v7x, 256 devices: a whole 4x4x8 slice. The times are simulated.
256 devices in a mesh: row: 2 (over core), col: 4 (over x), vis: 32 (over z, y).
Axes of the slice: x: 4, y: 4, z: 8, core: 2. Of those that a mesh axis runs over, the one named last changes fastest.
Arguments:
- text_embed: bfloat16 [32, 256, 5120], P('vis', None, 'row'), may hold values from -6 to 6
- image_embed: bfloat16 [32, 64, 5120], P('vis', 'col', 'row'), may hold values from -6 to 6
- slot_source: int32 [32, 256], replicated, may hold values from -1 to 2047, as said below
- segment_ids: int32 [32, 256], P('vis'), may hold values from 0 to 3, never falling along the last dimension, each value on 1 to 128 neighbouring positions
- prefix_lengths: int32 [32, 4], P('vis'), may hold values from 1 to 1024, 2048 in all within a row
- attn_gain: float32 [5120], P('row'), may hold values from 0.1 to 1.9
- qkv_weight: bfloat16 [5120, 3, 5120], P('row', None, 'col'), may hold values from -0.64286954 to 0.64286954
- out_weight: bfloat16 [5120, 5120], P('col', 'row'), may hold values from -0.5 to 0.5
- cache_keys: bfloat16 [32, 4, 1024, 5120], P('vis', None, 'row', 'col'), may hold values from -48 to 48
- cache_values: bfloat16 [32, 4, 1024, 5120], P('vis', None, 'row', 'col'), may hold values from -6 to 6
Outputs:
- hidden: float32 [32, 256, 5120], P('vis', 'col', 'row')
- new_keys: float32 [32, 256, 5120], P('vis', 'row', 'col')
- new_values: float32 [32, 256, 5120], P('vis', 'row', 'col')
- request_rms: float32 [32, 4], P('vis')
Inputs may be any that keep to these rules, and one draw needn't show every extreme that they name: `slot_source`: every global image index appears in exactly one slot; all other slots hold -1. The image tokens of one producing group fill at most 4 slots of any one group, and in every draw some group holds exactly 4 image tokens of every producing group.
All inputs are finite; a program needn't handle non-finite values.
Results may differ from a plain program's by a relative error of at most 0.012.
The roundings to bfloat16 on the way count: a program that leaves them out, or rounds other values in their place, can miss the bound.
Values may be sent and summed in bfloat16 or wider, within the bound.
A program may use at most 192 MiB of HBM per device.

v0:
```python
import jax
import jax.numpy as jnp
from jax import lax
from jax.sharding import PartitionSpec as P

D = 5120
HD = 128


EPSILON = 1e-06


def combined_all(value, axis, join):
    pieces = jax.tree.map(lambda part: lax.all_gather(part, axis), value)
    head = jax.tree.map(lambda part: part[0], pieces)
    tail = jax.tree.map(lambda part: part[1:], pieces)
    running, _ = lax.scan(lambda running, slab: (join(running, slab), None), head, tail)
    return running


def combine_parts(earlier_part, later_part):
    earlier_peak, earlier_sum, earlier_acc = earlier_part
    later_peak, later_sum, later_acc = later_part
    joint_peak = jnp.maximum(earlier_peak, later_peak)
    earlier_factor = jnp.exp(earlier_peak - joint_peak)
    later_factor = jnp.exp(later_peak - joint_peak)
    joint_sum = earlier_sum * earlier_factor + later_sum * later_factor
    joint_acc = earlier_acc * earlier_factor[..., None] + later_acc * later_factor[..., None]
    return (joint_peak, joint_sum, joint_acc)


def attend_block(queries, key_rows, value_rows, allowed):
    scores = jnp.einsum(
        "thd,khd->htk", queries, key_rows, preferred_element_type=jnp.float32
    ) * HD ** (-0.5)
    masked = jnp.where(allowed[None], scores, -1e30)
    peak_score = jnp.max(masked, axis=2)
    weights = jnp.where(allowed[None], jnp.exp(masked - peak_score[..., None]), 0.0)
    weight_sum = jnp.sum(weights, axis=2)
    summed = jnp.einsum(
        "htk,khd->htd", weights.astype(jnp.bfloat16), value_rows, preferred_element_type=jnp.float32
    )
    return (peak_score, weight_sum, summed)


def per_device(
    text_embed,
    image_embed,
    slot_source,
    segment_ids,
    prefix_lengths,
    attn_gain,
    qkv_weight,
    out_weight,
    cache_keys,
    cache_values,
):
    row_count = lax.axis_size("row")
    col_count = lax.axis_size("col")
    vis_count = lax.axis_size("vis")
    row_index = lax.axis_index("row")
    col_index = lax.axis_index("col")
    vis_index = lax.axis_index("vis")
    text_rows = text_embed[0]
    tokens_here = text_rows.shape[0]
    feature_width = text_rows.shape[1]
    sources = lax.dynamic_index_in_dim(slot_source, vis_index, 0, keepdims=False)
    pieces = lax.all_gather(image_embed, ("col", "vis"), axis=0, tiled=True)
    per_piece = pieces.shape[1]
    flat_rows = pieces.reshape(-1, feature_width)
    safe_index = jnp.maximum(sources, 0)
    group_size = per_piece * col_count
    group_of = safe_index // group_size
    within = safe_index % group_size
    located = (within // per_piece * vis_count + group_of) * per_piece + within % per_piece
    picked_rows = jnp.take(flat_rows, located, axis=0)
    filled = jnp.where((sources >= 0)[:, None], picked_rows, text_rows)
    wide_rows = filled.astype(jnp.float32)
    square_part = jnp.sum(wide_rows * wide_rows, axis=1)
    scaled = (wide_rows * attn_gain).astype(jnp.bfloat16)
    projected = jnp.einsum("td,dkh->tkh", scaled, qkv_weight, preferred_element_type=jnp.float32)
    blocks = tokens_here // row_count
    summed_all, square_sums = lax.psum((projected, square_part), "row")
    inv_rms = lax.rsqrt(square_sums / D + EPSILON)
    queries = (summed_all[:, 0] * inv_rms[:, None]).astype(jnp.bfloat16)
    pair_normed = summed_all[:, 1:] * inv_rms[:, None, None]
    pair_exact = lax.dynamic_slice_in_dim(pair_normed, row_index * blocks, blocks, 0)
    pair_mine = pair_exact.astype(jnp.bfloat16)
    head_width = queries.shape[1]
    heads_here = head_width // HD
    segments = segment_ids[0]
    lengths = prefix_lengths[0]
    request_count = lengths.shape[0]
    cache_block = cache_keys.shape[2]
    request_ids = jnp.arange(request_count, dtype=jnp.int32)
    cache_request = jnp.repeat(request_ids, cache_block)
    cache_position = row_index * cache_block + jnp.tile(
        jnp.arange(cache_block, dtype=jnp.int32), request_count
    )
    cache_ok = (cache_request[None, :] == segments[:, None]) & (
        cache_position < lengths[cache_request]
    )[None, :]
    token_ids = jnp.arange(tokens_here, dtype=jnp.int32)
    block_ids = row_index * blocks + jnp.arange(blocks, dtype=jnp.int32)
    block_segments = lax.dynamic_slice_in_dim(segments, row_index * blocks, blocks, 0)
    prompt_ok = (block_segments[None, :] == segments[:, None]) & (
        block_ids[None, :] <= token_ids[:, None]
    )
    allowed = jnp.concatenate([cache_ok, prompt_ok], axis=1)
    key_rows = jnp.concatenate(
        [cache_keys[0].reshape(-1, head_width), pair_mine[:, 0]], axis=0
    ).reshape(-1, heads_here, HD)
    value_rows = jnp.concatenate(
        [cache_values[0].reshape(-1, head_width), pair_mine[:, 1]], axis=0
    ).reshape(-1, heads_here, HD)
    local_parts = attend_block(
        queries.reshape(tokens_here, heads_here, HD), key_rows, value_rows, allowed
    )
    peak_score, weight_sum, summed = combined_all(local_parts, "row", combine_parts)
    attended = (
        (summed / weight_sum[..., None])
        .transpose(1, 0, 2)
        .reshape(tokens_here, head_width)
        .astype(jnp.bfloat16)
    )
    update = jnp.dot(attended, out_weight, preferred_element_type=jnp.float32)
    shares = lax.psum_scatter(update, "col", scatter_dimension=0, tiled=True)
    share_rows = tokens_here // col_count
    residual = lax.dynamic_slice_in_dim(wide_rows, col_index * share_rows, share_rows, 0)
    hidden = residual + shares
    onehot = (segments[None, :] == request_ids[:, None]).astype(jnp.float32)
    totals = jnp.dot(onehot, square_sums, precision=lax.Precision.HIGHEST)
    counts = jnp.sum(onehot, axis=1)
    request_rms = jnp.sqrt(totals / (counts * D))
    return (hidden[None], pair_exact[:, 0][None], pair_exact[:, 1][None], request_rms[None])


def solution(mesh):
    return jax.shard_map(
        per_device,
        mesh=mesh,
        in_specs=(
            P("vis", None, "row"),
            P("vis", "col", "row"),
            P(),
            P("vis", None),
            P("vis", None),
            P("row"),
            P("row", None, "col"),
            P("col", "row"),
            P("vis", None, "row", "col"),
            P("vis", None, "row", "col"),
        ),
        out_specs=(
            P("vis", "col", "row"),
            P("vis", "row", "col"),
            P("vis", "row", "col"),
            P("vis", None),
        ),
        check_vma=False,
    )
```

profile of v0, /device:TPU:2, one launch (start us, length us, event | category | flops | bytes accessed | tf_op | source)
XLA Modules:
  0.0 332.1 jit_solution(8110566947763616634)
XLA Ops:
  10.1 133.5 %all-gather.8.cloned.1.call-done = bf16[128,16,2560]{2,1,0:T(8,128)(2,1)} async-done(((bf16[1,16,2560]{2,1,0:T(8,128)(2,1)}), bf16[128,16,2560]{2,1,0:T(8,128)(2,1)}) %all-gather.8.cloned.1.call-update) | async-done | bytes 10485776 | tf_op jit(solution)/shard_map/all_gather | solution.py:68
  143.7 9.1 %gather_fusion = bf16[256,2560]{1,0:T(8,128)(2,1)} fusion(bf16[2048,2560]{1,0:T(8,128)(2,1)} %bitcast.111, s32[1024]{0:T(1024)S(1)} %pad_clamp_fusion), kind=kCustom, calls=%fused_computation | custom fusion | bytes 2622464 | tf_op jit(solution)/shard_map/jit(_take)/gather | solution.py:76
  152.8 2.4 multiply_reduce_fusion
  155.2 11.2 %fusion.14 = f32[256,3,1280]{2,0,1:T(8,128)} fusion(bf16[2560,3,1280]{2,0,1:T(8,128)(2,1)} %param.16, f32[256,2560]{1,0:T(8,128)S(1)} %get-tuple-element.33, f32[2560]{0:T(1024)S(1)} %copy-done.1), kind=kOutput, calls=%fused_computation.20 | convolution fusion | flops 5034475520 | bytes 26224640 | tf_op jit(solution)/shard_map/td,dkh->tkh/dot_general | solution.py:81
  166.6 11.3 %reshape.366 = bf16[2048,10,128]{2,1,0:T(8,128)(2,1)} reshape(bf16[1,4,512,1280]{3,2,1,0:T(8,128)(2,1)} %param.18) | data formatting | bytes 10485760 | tf_op jit(solution)/shard_map/concatenate | solution.py:110
  177.9 7.6 %copy.43 = bf16[2048,10,128]{2,0,1:T(8,128)(2,1)} copy(bf16[2048,10,128]{2,1,0:T(8,128)(2,1)} %reshape.366) | data formatting | bytes 10485760 | tf_op jit(solution)/shard_map/concatenate | solution.py:110
  185.5 11.4 %reshape.367 = bf16[2048,10,128]{2,1,0:T(8,128)(2,1)} reshape(bf16[1,4,512,1280]{3,2,1,0:T(8,128)(2,1)} %param.19) | data formatting | bytes 10485760 | tf_op jit(solution)/shard_map/concatenate | solution.py:113
  196.9 7.6 %copy.48 = bf16[2048,10,128]{2,0,1:T(8,128)(2,1)} copy(bf16[2048,10,128]{2,1,0:T(8,128)(2,1)} %reshape.367) | data formatting | bytes 10485760 | tf_op jit(solution)/shard_map/concatenate | solution.py:113
  205.1 2.6 compare_select_fusion.1
  208.3 2.7 psum.15
  211.1 2.5 slice.70
  213.6 2.8 copy.40
  226.0 14.4 %fusion = (f32[10,256]{1,0:T(8,128)S(1)}, f32[10,256,2176]{2,1,0:T(8,128)}) fusion(pred[256,2176]{1,0:T(8,128)(4,1)S(1)} %pad_add_fusion, bf16[128,10,128]{2,0,1:T(8,128)(2,1)S(1)} %copy.44, bf16[2048,10,128]{2,0,1:T(8,128)(2,1)} %copy.43, f32[256,10,128]{0,2,1:T(8,128)} %bitcast.113, f32[256]{0:T(256)S(1)} %add_rsqrt_fusion), kind=kOutput, calls=%fused_computation.3 | convolution fusion | flops 1454568960 | bytes 29731840 | tf_op jit(solution)/shard_map/thd,khd->htk/dot_general | solution.py:33
  240.4 13.0 %fusion.3 = f32[10,256,128]{2,1,0:T(8,128)} fusion(f32[10,256,2176]{2,1,0:T(8,128)} %get-tuple-element.47, f32[10,256]{1,0:T(8,128)S(1)} %get-tuple-element.46, pred[256,2176]{1,0:T(8,128)(4,1)S(1)} %pad_add_fusion, bf16[128,10,128]{2,0,1:T(8,128)(2,1)S(1)} %copy-done, bf16[2048,10,128]{2,0,1:T(8,128)(2,1)} %copy.48), kind=kOutput, calls=%fused_computation.6 | convolution fusion | flops 1465057280 | bytes 29730816 | tf_op jit(solution)/shard_map/htk,khd->htd/dot_general | solution.py:40
  255.3 11.6 %fusion.1 = f32[10,256]{1,0:T(8,128)S(1)} fusion(f32[10,256,2176]{2,1,0:T(8,128)} %get-tuple-element.47, f32[10,256]{1,0:T(8,128)S(1)} %get-tuple-element.46, pred[256,2176]{1,0:T(8,128)(4,1)S(1)} %pad_add_fusion), kind=kLoop, calls=%fused_computation.4 | loop fusion | flops 27850240 | bytes 22859776 | tf_op jit(solution)/shard_map/reduce_sum | solution.py:39
  266.9 2.1 all-gather.4
  269.6 3.5 %fusion.44 = (f32[10,256,128]{2,1,0:T(8,128)}, f32[10,256,128]{2,1,0:T(8,128)}) fusion(f32[20,256,128]{2,1,0:T(8,128)} %all-gather.10.cloned.1.call-done), kind=kLoop, calls=%fused_computation.97 | loop fusion | bytes 5242880 | tf_op jit(solution)/shard_map/slice | solution.py:15
  273.1 2.8 copy.57
  275.9 2.8 copy.58
  278.7 2.0 divide_convert_fusion
  280.6 6.3 %fusion.47 = f32[256,2560]{1,0:T(8,128)} fusion(bf16[256,1280]{0,1:T(8,128)(2,1)S(1)} %bitcast.112, bf16[1280,2560]{1,0:T(8,128)(2,1)} %param.17), kind=kOutput, calls=%fused_computation.100 | convolution fusion | flops 1677721600 | bytes 9830400 | tf_op jit(solution)/shard_map/dot_general | solution.py:126
  287.7 2.4 slice_bitcast_fusion
  290.1 33.5 %reduce-scatter.2.cloned.1.call-done = f32[64,2560]{1,0:T(8,128)} async-done(((f32[256,2560]{1,0:T(8,128)}), f32[64,2560]{1,0:T(8,128)}) %reduce-scatter.2.cloned.1.call-update) | async-done | bytes 655376 | tf_op jit(solution)/shard_map/reduce_scatter | solution.py:127
  323.6 2.0 add_bitcast_fusion
  (50 shorter events, 17.3 us)
Async XLA Ops:
  7.2 136.5 %all-gather.8.cloned.1.call-start = ((), (), s32[]{:S(2)}) async-start(), calls=%async_computation.1 | async-start | bytes 10567680 | tf_op jit(solution)/shard_map/all_gather | solution.py:68
  7.9 203.2 %all-reduce.2.cloned.1.call-start = ((), (), s32[]{:S(2)}) async-start(), calls=%async_computation.2 | async-start | bytes 7864320 | tf_op jit(solution)/shard_map/psum | solution.py:83
  152.8 2.4 copy-start.1
  166.5 103.2 %all-gather.10.cloned.1.call-start = ((), (), s32[]{:S(2)}) async-start(), calls=%async_computation.4 | async-start | bytes 3932160 | tf_op jit(solution)/shard_map/all_gather | solution.py:14
  196.9 7.6 %copy-start.2 = (s32[1,4]{1,0:T(1,128)S(1)}, s32[1,4]{1,0:T(1,128)}, u32[]{:S(2)}) copy-start(s32[1,4]{1,0:T(1,128)} %param.14) | copy-start | bytes 52
  196.9 10.8 %copy-start.3 = (s32[1,256]{1,0:T(1,128)S(1)}, s32[1,256]{1,0:T(1,128)}, u32[]{:S(2)}) copy-start(s32[1,256]{1,0:T(1,128)} %param.13) | copy-start | bytes 3076
  216.3 1.7 slice-start
  225.9 14.4 %copy-start = (bf16[128,10,128]{2,0,1:T(8,128)(2,1)S(1)}, bf16[128,10,128]{2,0,1:T(8,128)(2,1)}, u32[]{:S(2)}) copy-start(bf16[128,10,128]{2,0,1:T(8,128)(2,1)} %copy.49) | copy-start | bytes 983044
  253.4 70.2 %reduce-scatter.2.cloned.1.call-start = ((), (), s32[]{:S(2)}) async-start(), calls=%async_computation.3 | async-start | bytes 3276800 | tf_op jit(solution)/shard_map/reduce_scatter | solution.py:127
Sparse Core Ops, SparseCore 0:
  11.5 132.1 all-gather.7
  166.6 33.1 all-reduce.1
  253.5 16.0 all-gather.9
  287.0 36.5 reduce-scatter.1
where the time goes:
time: 336 us; the launch traced here: 332 us
  waiting for transfers between devices  168 us (50%)
  local copies, waits for them, and re-layouts  72.8 us (22%)
  matrix products  45.5 us (14%)
  other arithmetic  24.7 us (7%)
  between operations  13.9 us (4%)
  blocking collectives  6.55 us (2%)
    all_gather x1, waiting for transfers between devices, per_device(): pieces = lax.all_gather(image_embed, ('col', 'vis'), axis=0, tiled=True)  134 us
    reduce_scatter x1, waiting for transfers between devices, per_device(): shares = lax.psum_scatter(update, 'col', scatter_dimension=0, tiled=True)  33.5 us
    concatenate x3, local copies, waits for them, and re-layouts, per_device(): jnp.concatenate([cache_values[0].reshape(-1, head_width), pair_mine[:, 1]...  20.8 us
    concatenate x3, local copies, waits for them, and re-layouts, per_device(): jnp.concatenate([cache_keys[0].reshape(-1, head_width), pair_mine[:, 0]],...  20.1 us
    dot_general x1, matrix products, attend_block(): jnp.einsum('thd,khd->htk', queries, key_rows, preferred_element_type=jnp....  14.4 us
    dot_general x1, matrix products, attend_block(): jnp.einsum('htk,khd->htd', weights.astype(jnp.bfloat16), value_rows, pref...  13 us
    reduce_sum x1, other arithmetic, attend_block(): weight_sum = jnp.sum(weights, axis=2)  11.6 us
    dot_general x1, matrix products, per_device(): jnp.einsum('td,dkh->tkh', scaled, qkv_weight, preferred_element_type=jnp....  11.2 us
  transfers between devices with their start and end apart: 4, of which 3 were waited for; matrix products, arithmetic and copies ran while one was open for 18% of the time, Pallas kernels for 0%

commit v1 on v0

v1 whole, which is shorter than its diff:
```python
import functools

import jax
import jax.numpy as jnp
from jax import lax
from jax.experimental import pallas as pl
from jax.experimental.pallas import tpu as pltpu
from jax.sharding import PartitionSpec as P

D = 5120
HD = 128
EPSILON = 1e-06
MASKED = -1e30
SCALE_LOG2E = HD ** (-0.5) * 1.4426950408889634

MESH = pl.DeviceIdType.MESH
F32 = jnp.float32
BF16 = jnp.bfloat16

COLS = 4
ZS = 8
YS = 4
TOK = 256
FEAT = 2560
QUART = 640
WIDTH = 1280
HEADS_HERE = 10
CACHE = 512
REQS = 4
HALF = 128
SHARE = 64
TILE = 512
TILES = FEAT // TILE
Z_ORDER = (1, 7, 2, 6, 3, 5, 4)


def nt_dot(left, right):
    return lax.dot_general(left, right, (((1,), (1,)), ((), ())), preferred_element_type=F32)


def nn_dot(left, right):
    return jnp.dot(left, right, preferred_element_type=F32)


def kernel(
    text_hbm, image_hbm, slots_ref, seg_ref, lens_ref, gain_ref, w_hbm, ow_hbm, ck_hbm, cv_hbm,
    hid_hbm, nk_hbm, nv_hbm, rms_ref,
    w, ow, ck, cv, fill, gath, zsend, compact, scaled,
    sq_own, sq_peer, inv, kv_own, kv_send, kv_recv, q_own, q_send, q_recv, q_bf, kv_bf, kv_out,
    ext, onehot, bias, scores, o_own, o_peer, st_own, st_peer, att,
    upd, hop_a, hop_b, got_a, got_b, out_l, out_r, fin_l, fin_r, hid,
    w_sem, in_sem, out_sem, xy_send, xy_recv, z_send, z_recv, x_send, x_recv,
    pr_send, pr_recv, o_send, o_recv, r_send, r_recv,
):
    row = lax.axis_index("row")
    col = lax.axis_index("col")
    vis = lax.axis_index("vis")
    z = lax.div(vis, YS)
    y = lax.rem(vis, YS)
    other = 1 - row
    right = lax.rem(col + 1, COLS)
    left = lax.rem(col + COLS - 1, COLS)
    across = lax.rem(col + 2, COLS)

    def at(r, c, v):
        return (r, c, v)

    loads_w = []
    for j in (1, 2, 0):
        for part in range(4):
            rows = pl.ds(part * QUART, QUART)
            cp = pltpu.make_async_copy(w_hbm.at[j, rows], w.at[j, rows], w_sem.at[j * 4 + part])
            loads_w.append((j, cp))
    load_text = pltpu.make_async_copy(text_hbm, fill, in_sem.at[0])
    load_k = [pltpu.make_async_copy(ck_hbm.at[s], ck.at[s], in_sem.at[1 + s]) for s in range(REQS)]
    load_v = [pltpu.make_async_copy(cv_hbm.at[s], cv.at[s], in_sem.at[5 + s]) for s in range(REQS)]
    load_ow = [
        pltpu.make_async_copy(ow_hbm.at[pl.ds(p * 320, 320)], ow.at[pl.ds(p * 320, 320)], in_sem.at[9 + p])
        for p in range(4)
    ]
    block = y * COLS + col
    own_rows = pl.ds(pl.multiple_of(block * 16, 16), 16)
    own_cols = pl.ds(pl.multiple_of(col * QUART, 128), QUART)
    load_own = pltpu.make_async_copy(image_hbm.at[:, own_cols], gath.at[own_rows], in_sem.at[13])
    load_own.start()
    load_text.start()

    barrier = pltpu.get_barrier_semaphore()
    for step in range(1, 16):
        to = lax.rem(block + step, 16)
        pl.semaphore_signal(
            barrier, inc=1, device_id=at(row, lax.rem(to, COLS), z * YS + lax.div(to, COLS)), device_id_type=MESH)
    for step in range(1, ZS):
        pl.semaphore_signal(
            barrier, inc=1, device_id=at(row, col, lax.rem(z + step, ZS) * YS + y), device_id_type=MESH)
    pl.semaphore_signal(barrier, inc=1, device_id=at(other, col, vis), device_id_type=MESH)
    for _, cp in loads_w:
        cp.start()

    lane256 = lax.broadcasted_iota(jnp.int32, (128, TOK), 1)
    sub128 = lax.broadcasted_iota(jnp.int32, (128, TOK), 0)
    before = jnp.where(
        lax.broadcasted_iota(jnp.int32, (TOK, TOK), 0) < lax.broadcasted_iota(jnp.int32, (TOK, TOK), 1), 1.0, 0.0
    ).astype(BF16)
    to_rows = jnp.concatenate(
        [jnp.broadcast_to(slots_ref[pl.ds(zz * YS + y, 1), :], (16, TOK)) for zz in range(ZS)], axis=0)
    rank_of = sub128 & 3
    match = (to_rows >> 6) == (z * YS + ((sub128 & 15) >> 2))
    earlier = nn_dot(jnp.where(match, 1.0, 0.0).astype(BF16), before)
    chosen = match & (earlier.astype(jnp.int32) == rank_of)
    token_at = jnp.sum(
        jnp.where(chosen, (to_rows - z * TOK + 1).astype(F32), 0.0), axis=1, keepdims=True).astype(jnp.int32) - 1
    select = jnp.where(token_at == lane256, 1.0, 0.0).astype(BF16)

    here_rows = jnp.broadcast_to(slots_ref[pl.ds(vis, 1), :], (128, TOK))
    here = (here_rows >> 6) == (sub128 >> 2)
    here_before = nn_dot(jnp.where(here, 1.0, 0.0).astype(BF16), before)
    place_f = jnp.where(here & (here_before.astype(jnp.int32) == rank_of), 1.0, 0.0).T
    place = place_f.astype(BF16)
    has_image = jnp.sum(place_f, axis=1, keepdims=True)

    seg_rows = jnp.broadcast_to(seg_ref[...], (128, TOK))
    oh = jnp.where(seg_rows == sub128, 1.0, 0.0).T
    onehot[...] = oh.astype(BF16)
    lane128 = lax.broadcasted_iota(jnp.int32, (TOK, HALF), 1)
    tok128 = lax.broadcasted_iota(jnp.int32, (TOK, HALF), 0)
    seg_col = jnp.sum(oh * lane128.astype(F32), axis=1, keepdims=True).astype(jnp.int32)
    seg_mine = jnp.where(row == 0, seg_ref[:, :HALF], seg_ref[:, HALF:])
    bias[...] = jnp.where(
        (seg_col == seg_mine) & (lane128 + row * HALF <= tok128), 0.0, MASKED)
    for s in range(REQS):
        lane_c = lax.broadcasted_iota(jnp.int32, (CACHE, HD), 1)
        pos = lax.broadcasted_iota(jnp.int32, (CACHE, HD), 0) + row * CACHE
        seen = (lane_c == s) & (pos < lens_ref[0, s])
        ext[s] = jnp.where(seen | (lane_c >= REQS), 0.0, MASKED).astype(BF16)

    pl.semaphore_wait(barrier, 23)
    for step in range(1, 16):
        to = lax.rem(block + step, 16)
        to_col = lax.rem(to, COLS)
        pltpu.make_async_remote_copy(
            src_ref=image_hbm.at[:, pl.ds(pl.multiple_of(to_col * QUART, 128), QUART)],
            dst_ref=gath.at[own_rows],
            send_sem=xy_send.at[step], recv_sem=xy_recv.at[step],
            device_id=at(row, to_col, z * YS + lax.div(to, COLS)), device_id_type=MESH).start()
    for group in (load_k, load_v, load_ow):
        for cp in group:
            cp.start()
    load_own.wait()
    for step in range(1, 16):
        frm = lax.rem(block + 16 - step, 16)
        rows = pl.ds(pl.multiple_of(frm * 16, 16), 16)
        pltpu.make_async_remote_copy(
            src_ref=gath.at[rows], dst_ref=gath.at[rows],
            send_sem=xy_send.at[step], recv_sem=xy_recv.at[step],
            device_id=at(row, col, vis), device_id_type=MESH).wait_recv()

    def block_at(dz, c_src):
        zz = lax.rem(z + dz, ZS)
        return compact.at[pl.ds(pl.multiple_of(zz * 16, 16), 16), pl.ds(pl.multiple_of(c_src * QUART, 128), QUART)]

    zsend[...] = nn_dot(select, gath[...]).astype(BF16)
    for dz in Z_ORDER:
        zz = lax.rem(z + dz, ZS)
        pltpu.make_async_remote_copy(
            src_ref=zsend.at[pl.ds(pl.multiple_of(zz * 16, 16), 16)],
            dst_ref=block_at(0, col),
            send_sem=z_send.at[dz], recv_sem=z_recv.at[ZS - dz],
            device_id=at(row, col, zz * YS + y), device_id_type=MESH).start()

    def x_copy(dz, c_src, to_col, lane):
        return pltpu.make_async_remote_copy(
            src_ref=block_at(dz, c_src), dst_ref=block_at(dz, c_src),
            send_sem=x_send.at[dz, lane], recv_sem=x_recv.at[dz, lane],
            device_id=at(row, to_col, vis), device_id_type=MESH)

    def z_wait(dz):
        pltpu.make_async_remote_copy(
            src_ref=block_at(dz, col), dst_ref=block_at(dz, col),
            send_sem=z_send.at[dz], recv_sem=z_recv.at[dz],
            device_id=at(row, col, vis), device_id_type=MESH).wait_recv()

    order = (0,) + Z_ORDER
    for i, dz in enumerate(order):
        if dz == 0:
            block_own = pltpu.make_async_copy(
                zsend.at[pl.ds(pl.multiple_of(z * 16, 16), 16)], block_at(0, col), in_sem.at[14])
            block_own.start()
            block_own.wait()
        else:
            z_wait(dz)
        x_copy(dz, col, right, 0).start()
        x_copy(dz, col, left, 1).start()
        if i >= 1:
            forward(x_copy, order[i - 1], i - 1, left, right)
    forward(x_copy, order[-1], len(order) - 1, left, right)
    for i, dz in enumerate(order):
        if i % 2 == 0:
            x_copy(dz, right, left, 1).wait_recv()
        else:
            x_copy(dz, left, right, 0).wait_recv()
        x_copy(dz, across, left, 2).wait_recv()

    load_text.wait()
    squares = jnp.zeros((TOK, HD), F32)
    for n in range(TILES):
        cols = slice(n * TILE, (n + 1) * TILE)
        picked = nn_dot(place, compact[:, cols])
        rows_f = jnp.where(has_image > 0.0, picked, fill[:, cols].astype(F32))
        fill[:, cols] = rows_f.astype(BF16)
        scaled[:, cols] = (rows_f * gain_ref[:, cols]).astype(BF16)
        for k in range(TILE // HD):
            piece = rows_f[:, k * HD:(k + 1) * HD]
            squares = squares + piece * piece
    sq_own[...] = jnp.broadcast_to(jnp.sum(squares, axis=1, keepdims=True), (TOK, HD))

    def to_peer(src, dst, k):
        return pltpu.make_async_remote_copy(
            src_ref=src, dst_ref=dst, send_sem=pr_send.at[k], recv_sem=pr_recv.at[k],
            device_id=at(other, col, vis), device_id_type=MESH)

    sq_copy = to_peer(sq_own, sq_peer, 0)
    sq_copy.start()

    peer_copies = {}
    for j in (1, 2, 0):
        for jj, cp in loads_w:
            if jj == j:
                cp.wait()
        if j == 0:
            def q_body(n, carry):
                lanes = pl.ds(pl.multiple_of(n * 256, 256), 256)
                part = nn_dot(scaled[...], w[0, :, lanes])
                q_own[:, lanes] = part
                q_send[:, lanes] = part.astype(BF16)
                return carry
            lax.fori_loop(0, 5, q_body, 0)
            peer_copies[j] = to_peer(q_send, q_recv, 3)
        else:
            def kv_body(n, carry, j=j):
                lanes = pl.ds(pl.multiple_of(n * 256, 256), 256)
                part = nn_dot(scaled[...], w[j, :, lanes])
                kv_own[j - 1, :, lanes] = jnp.where(row == 0, part[:HALF], part[HALF:])
                kv_send[j - 1, :, lanes] = jnp.where(row == 0, part[HALF:], part[:HALF]).astype(BF16)
                return carry
            lax.fori_loop(0, 5, kv_body, 0)
            peer_copies[j] = to_peer(kv_send.at[j - 1], kv_recv.at[j - 1], j)
        peer_copies[j].start()

    sq_copy.wait()
    total_sq = sq_own[...] + sq_peer[...]
    inv[...] = lax.rsqrt(total_sq / D + EPSILON)
    per_request = jnp.sum(oh * total_sq, axis=0, keepdims=True)
    counts = jnp.sum(oh, axis=0, keepdims=True)
    rms_ref[...] = jnp.sqrt(per_request / (counts * D))[:, :REQS]
    inv_mine = inv[pl.ds(pl.multiple_of(row * HALF, HALF), HALF), :]
    outs = []
    for j, dst in ((1, nk_hbm), (2, nv_hbm)):
        peer_copies[j].wait()
        for h in range(HEADS_HERE):
            lanes = slice(h * HD, (h + 1) * HD)
            value = (kv_own[j - 1, :, lanes] + kv_recv[j - 1, :, lanes].astype(F32)) * inv_mine
            kv_out[j - 1, :, lanes] = value
            kv_bf[j - 1, :, lanes] = value.astype(BF16)
        cp = pltpu.make_async_copy(kv_out.at[j - 1], dst, out_sem.at[j])
        cp.start()
        outs.append(cp)
    peer_copies[0].wait()
    for h in range(HEADS_HERE):
        lanes = slice(h * HD, (h + 1) * HD)
        q_bf[:, lanes] = ((q_own[:, lanes] + q_recv[:, lanes].astype(F32)) * inv[...]).astype(BF16)

    for group in (load_k, load_v):
        for cp in group:
            cp.wait()
    st_own[...] = jnp.zeros((TOK, HD), F32)

    def o_copy(h):
        lanes = pl.ds(pl.multiple_of(h * HD, HD), HD)
        return pltpu.make_async_remote_copy(
            src_ref=o_own.at[:, lanes], dst_ref=o_peer.at[:, lanes],
            send_sem=o_send.at[h], recv_sem=o_recv.at[h],
            device_id=at(other, col, vis), device_id_type=MESH)

    def head(h, carry):
        lanes = pl.ds(pl.multiple_of(h * HD, HD), HD)
        q = q_bf[:, lanes]
        q_ext = jnp.concatenate([q, onehot[...]], axis=1)
        new = nt_dot(q, kv_bf[0, :, lanes]) + bias[...]
        scores[:, REQS * CACHE:] = new
        peak = new
        for s in range(REQS):
            part = nt_dot(q_ext, jnp.concatenate([ck[s, :, lanes], ext[s]], axis=1))
            scores[:, s * CACHE:(s + 1) * CACHE] = part
            for k in range(CACHE // HD):
                peak = jnp.maximum(peak, part[:, k * HD:(k + 1) * HD])
        top = jnp.max(peak, axis=1, keepdims=True) * SCALE_LOG2E
        ones = jnp.ones((CACHE, HD), BF16)
        weights = jnp.exp2(scores[:, REQS * CACHE:] * SCALE_LOG2E - top).astype(BF16)
        acc = nn_dot(weights, jnp.concatenate([kv_bf[1, :, lanes], ones[:HALF]], axis=1))
        for s in range(REQS):
            weights = jnp.exp2(scores[:, s * CACHE:(s + 1) * CACHE] * SCALE_LOG2E - top).astype(BF16)
            acc = acc + nn_dot(weights, jnp.concatenate([cv[s, :, lanes], ones], axis=1))
        total = acc[:, HD:]
        o_own[:, lanes] = (acc[:, :HD] / total).astype(BF16)
        st_own[...] = jnp.where(lane128 == h, top + jnp.log2(total), st_own[...])
        o_copy(h).start()
        return carry

    lax.fori_loop(0, HEADS_HERE, head, 0)
    st_copy = to_peer(st_own, st_peer, 4)
    st_copy.start()
    st_copy.wait()
    lead = st_own[...] - st_peer[...]
    mine = 1.0 / (1.0 + jnp.exp2(-lead))
    theirs = 1.0 / (1.0 + jnp.exp2(lead))
    for h in range(HEADS_HERE):
        lanes = slice(h * HD, (h + 1) * HD)
        o_copy(h).wait()
        att[:, lanes] = (
            o_own[:, lanes].astype(F32) * mine[:, h:h + 1] + o_peer[:, lanes].astype(F32) * theirs[:, h:h + 1]
        ).astype(BF16)

    for cp in load_ow:
        cp.wait()

    def share(c):
        return pl.ds(pl.multiple_of(c * SHARE, SHARE), SHARE)

    def ring(src, dst, k, lane, to_col):
        return pltpu.make_async_remote_copy(
            src_ref=src, dst_ref=dst, send_sem=r_send.at[k, lane], recv_sem=r_recv.at[k, lane],
            device_id=at(row, to_col, vis), device_id_type=MESH)

    def hop(n):
        return (
            ring(hop_a.at[n], got_a.at[n], n, 0, right),
            ring(hop_b.at[n], got_b.at[n], n, 1, left),
        )

    def last(n):
        return (
            ring(out_r.at[n], fin_l.at[n], n, 2, right),
            ring(out_l.at[n], fin_r.at[n], n, 3, left),
        )

    half = TILE // 2

    def second(n):
        one, two = hop(n)
        cols = pl.ds(n * TILE, TILE)
        one.wait_recv()
        two.wait_recv()
        to_right = upd[share(right), cols]
        out_r[n] = jnp.concatenate(
            [to_right[:, :half] + got_a[n].astype(F32), to_right[:, half:]], axis=1).astype(BF16)
        to_left = upd[share(left), cols]
        out_l[n] = jnp.concatenate(
            [to_left[:, :half], to_left[:, half:] + got_b[n].astype(F32)], axis=1).astype(BF16)
        for cp in last(n):
            cp.start()

    for n in range(TILES):
        cols = pl.ds(n * TILE, TILE)
        upd[:, cols] = nn_dot(att[...], ow[:, cols])
        far = upd[share(across), cols]
        hop_a[n] = far[:, :half].astype(BF16)
        hop_b[n] = far[:, half:].astype(BF16)
        for cp in hop(n):
            cp.start()
        if n >= 1:
            second(n - 1)
    second(TILES - 1)
    for n in range(TILES):
        cols = pl.ds(n * TILE, TILE)
        for cp in last(n):
            cp.wait_recv()
        hid[:, cols] = (
            fill[share(col), cols].astype(F32) + upd[share(col), cols]
            + (fin_l[n].astype(F32) + fin_r[n].astype(F32)))
        cp = pltpu.make_async_copy(hid.at[:, cols], hid_hbm.at[:, cols], out_sem.at[3 + n])
        cp.start()
        outs.append(cp)

    for step in range(1, 16):
        pltpu.make_async_remote_copy(
            src_ref=image_hbm.at[:, own_cols], dst_ref=gath.at[own_rows],
            send_sem=xy_send.at[step], recv_sem=xy_recv.at[step],
            device_id=at(other, col, vis), device_id_type=MESH).wait_send()
    for dz in Z_ORDER:
        pltpu.make_async_remote_copy(
            src_ref=zsend.at[pl.ds(0, 16)], dst_ref=block_at(0, col),
            send_sem=z_send.at[dz], recv_sem=z_recv.at[dz],
            device_id=at(other, col, vis), device_id_type=MESH).wait_send()
    for dz in order:
        for lane in range(3):
            x_copy(dz, col, right, lane).wait_send()
    for n in range(TILES):
        for cp in hop(n) + last(n):
            cp.wait_send()
    for cp in outs:
        cp.wait()


def forward(x_copy, dz, i, left, right):
    if i % 2 == 0:
        x_copy(dz, left, right, 0).wait_recv()
        x_copy(dz, left, right, 2).start()
    else:
        x_copy(dz, right, left, 1).wait_recv()
        x_copy(dz, right, left, 2).start()


def per_device(
    text_embed, image_embed, slot_source, segment_ids, prefix_lengths,
    attn_gain, qkv_weight, out_weight, cache_keys, cache_values,
):
    hbm = pl.BlockSpec(memory_space=pl.ANY)
    vmem = pl.BlockSpec(memory_space=pltpu.VMEM)
    smem = pl.BlockSpec(memory_space=pltpu.SMEM)

    def v(shape, dtype):
        return pltpu.VMEM(shape, dtype)

    dma = pltpu.SemaphoreType.DMA
    hidden, keys, values, rms = pl.pallas_call(
        kernel,
        out_shape=(
            jax.ShapeDtypeStruct((SHARE, FEAT), F32),
            jax.ShapeDtypeStruct((HALF, WIDTH), F32),
            jax.ShapeDtypeStruct((HALF, WIDTH), F32),
            jax.ShapeDtypeStruct((1, REQS), F32),
        ),
        in_specs=[hbm, hbm, vmem, vmem, smem, vmem, hbm, hbm, hbm, hbm],
        out_specs=(hbm, hbm, hbm, vmem),
        scratch_shapes=[
            v((3, FEAT, WIDTH), BF16), v((WIDTH, FEAT), BF16),
            v((REQS, CACHE, WIDTH), BF16), v((REQS, CACHE, WIDTH), BF16),
            v((TOK, FEAT), BF16), v((TOK, QUART), BF16), v((HALF, QUART), BF16), v((HALF, FEAT), BF16),
            v((TOK, FEAT), BF16),
            v((TOK, HD), F32), v((TOK, HD), F32), v((TOK, HD), F32),
            v((2, HALF, WIDTH), F32), v((2, HALF, WIDTH), BF16), v((2, HALF, WIDTH), BF16),
            v((TOK, WIDTH), F32), v((TOK, WIDTH), BF16), v((TOK, WIDTH), BF16), v((TOK, WIDTH), BF16),
            v((2, HALF, WIDTH), BF16), v((2, HALF, WIDTH), F32),
            v((REQS, CACHE, HD), BF16), v((TOK, HD), BF16), v((TOK, HALF), F32),
            v((TOK, REQS * CACHE + HALF), F32),
            v((TOK, WIDTH), BF16), v((TOK, WIDTH), BF16), v((TOK, HD), F32), v((TOK, HD), F32),
            v((TOK, WIDTH), BF16),
            v((TOK, FEAT), F32),
            v((TILES, SHARE, TILE // 2), BF16), v((TILES, SHARE, TILE // 2), BF16),
            v((TILES, SHARE, TILE // 2), BF16), v((TILES, SHARE, TILE // 2), BF16),
            v((TILES, SHARE, TILE), BF16), v((TILES, SHARE, TILE), BF16),
            v((TILES, SHARE, TILE), BF16), v((TILES, SHARE, TILE), BF16),
            v((SHARE, FEAT), F32),
            dma((12,)), dma((15,)), dma((8,)), dma((16,)), dma((16,)), dma((8,)), dma((8,)),
            dma((8, 3)), dma((8, 3)), dma((5,)), dma((5,)), dma((HEADS_HERE,)), dma((HEADS_HERE,)),
            dma((TILES, 4)), dma((TILES, 4)),
        ],
        compiler_params=pltpu.CompilerParams(
            collective_id=0, has_side_effects=True, vmem_limit_bytes=60 * 1024 * 1024),
    )(
        text_embed[0], image_embed[0], slot_source, segment_ids, prefix_lengths,
        attn_gain.reshape(1, -1), qkv_weight.transpose(1, 0, 2), out_weight, cache_keys[0], cache_values[0],
    )
    return hidden[None], keys[None], values[None], rms


def solution(mesh):
    return jax.shard_map(
        per_device,
        mesh=mesh,
        in_specs=(
            P("vis", None, "row"),
            P("vis", "col", "row"),
            P(),
            P("vis", None),
            P("vis", None),
            P("row"),
            P("row", None, "col"),
            P("col", "row"),
            P("vis", None, "row", "col"),
            P("vis", None, "row", "col"),
        ),
        out_specs=(
            P("vis", "col", "row"),
            P("vis", "row", "col"),
            P("vis", "row", "col"),
            P("vis", None),
        ),
        check_vma=False,
    )
```

time: 336 us -> 94.5 us (0.28); the launches traced: 332 us -> 94.2 us
  waiting for transfers between devices: 168 us -> 0 us
  Pallas kernels: 0 us -> 85.1 us
  local copies, waits for them, and re-layouts: 72.8 us -> 8.39 us
  matrix products: 45.5 us -> 0 us
  other arithmetic: 24.7 us -> 0 us
  between operations: 13.9 us -> 0.64 us
  blocking collectives: 6.55 us -> 0 us
    all_gather x2 -> x0, waiting for transfers between devices: 134 us -> none  [the longest x1 134 us: per_device(): pieces = lax.all_gather(image_embed, ('col', 'vis'), axis=0, tiled=True)]
    pallas_call x0 -> x1, Pallas kernels: none -> 85.1 us  [per_device(): pl.pallas_call(kernel, out_shape=(jax.ShapeDtypeStruct((SHARE, FEAT), F32...]
    dot_general x5 -> x0, matrix products: 45.5 us -> none  [the longest x1 14.4 us: attend_block(): jnp.einsum('thd,khd->htk', queries, key_rows, preferred_element_type=jnp....]
    concatenate x6 -> x0, local copies, waits for them, and re-layouts: 40.9 us -> none  [the longest x3 20.8 us: per_device(): jnp.concatenate([cache_values[0].reshape(-1, head_width), pair_mine[:, 1]...]
    reduce_scatter x1 -> x0, waiting for transfers between devices: 33.5 us -> none  [per_device(): shares = lax.psum_scatter(update, 'col', scatter_dimension=0, tiled=True)]
    reduce_sum x3 -> x0, other arithmetic: 14.1 us -> none  [the longest x1 11.6 us: attend_block(): weight_sum = jnp.sum(weights, axis=2)]
    slice x8 -> x0, local copies, waits for them, and re-layouts: 14 us -> none  [the longest x2 5.27 us: per_device(): queries = (summed_all[:, 0] * inv_rms[:, None]).astype(jnp.bfloat16)]
    gather x2 -> x0, local copies, waits for them, and re-layouts: 9.73 us -> none  [the longest x1 9.14 us: per_device(): picked_rows = jnp.take(flat_rows, located, axis=0)]
  transfers between devices with their start and end apart: 4 -> 0, of which waited for: 3 -> 0; matrix products, arithmetic and copies ran while one was open for 18% -> 0% of each run, Pallas kernels for 0% -> 0%
where the time goes in v1:
time: 94.5 us; the launch traced here: 94.2 us
  Pallas kernels  85.1 us (90%)
  local copies, waits for them, and re-layouts  8.39 us (9%)
    pallas_call x1, Pallas kernels, per_device(): pl.pallas_call(kernel, out_shape=(jax.ShapeDtypeStruct((SHARE, FEAT), F32...  85.1 us
    unnamed x4, local copies, waits for them, and re-layouts  7.08 us

profile of v1, /device:TPU:2, one launch (start us, length us, event | category | flops | bytes accessed | tf_op | source)
XLA Modules:
  0.0 94.2 jit_solution(2390131830976071234)
XLA Ops:
  0.6 1.3 %reshape.11.gain_ref = f32[1,2560]{1,0:T(1,128)} reshape(f32[2560]{0:T(1024)} %param.15) | data formatting | bytes 20480 | tf_op jit(solution)/shard_map/reshape | solution.py:463
  1.9 85.1 %shard_map.129 = (f32[64,2560]{1,0:T(8,128)}, f32[128,1280]{1,0:T(8,128)}, f32[128,1280]{1,0:T(8,128)}, f32[1,4]{1,0:T(1,128)}) custom-call(bf16[256,2560]{1,0:T(8,128)(2,1)} %bitcast.11, bf16[16,2560]{1,0:T(8,128)(2,1)} %bitcast.15, s32[32,256]{1,0:T(8,128)} %slots_ref.1, s32[1,256]{1,0:T(1,128)} %seg_ref.1, s32[1,4]{1,0:T(1,128)} %lens_ref.1, ...), custom_call_target="tpu_custom_call" | custom-call | tf_op jit(solution)/shard_map/pallas_call | solution.py:426
  87.1 2.0 %copy.18 = f32[1,64,2560]{2,1,0:T(8,128)} copy(f32[1,64,2560]{2,1,0:T(8,128)} %bitcast.14) | data formatting | bytes 1310720
  89.0 2.0 %copy.19 = f32[1,128,1280]{2,1,0:T(8,128)} copy(f32[1,128,1280]{2,1,0:T(8,128)} %bitcast.13) | data formatting | bytes 1310720
  91.0 2.0 %copy.20 = f32[1,128,1280]{2,1,0:T(8,128)} copy(f32[1,128,1280]{2,1,0:T(8,128)} %bitcast.12) | data formatting | bytes 1310720
  93.0 1.2 %copy.21 = f32[1,4]{1,0:T(1,128)} copy(f32[1,4]{1,0:T(1,128)} %get-tuple-element.19) | data formatting | bytes 32

commit v2 on v1

v2 whole, which is shorter than its diff:
```python
import functools

import jax
import jax.numpy as jnp
from jax import lax
from jax.experimental import pallas as pl
from jax.experimental.pallas import tpu as pltpu
from jax.sharding import PartitionSpec as P

D = 5120
HD = 128
EPSILON = 1e-06
MASKED = -1e30
SCALE_LOG2E = HD ** (-0.5) * 1.4426950408889634

MESH = pl.DeviceIdType.MESH
F32 = jnp.float32
BF16 = jnp.bfloat16

COLS = 4
ZS = 8
YS = 4
TOK = 256
FEAT = 2560
QUART = 640
WIDTH = 1280
HEADS_HERE = 10
CACHE = 512
REQS = 4
HALF = 128
SHARE = 64
TILE = 512
TILES = FEAT // TILE
Z_ORDER = (1, 7, 2, 6, 3, 5, 4)


def nt_dot(left, right):
    return lax.dot_general(left, right, (((1,), (1,)), ((), ())), preferred_element_type=F32)


def nn_dot(left, right):
    return jnp.dot(left, right, preferred_element_type=F32)


def kernel(
    text_hbm, image_hbm, slots_ref, seg_ref, lens_ref, gain_ref, w_hbm, ow_hbm, ck_hbm, cv_hbm,
    hid_hbm, nk_hbm, nv_hbm, rms_ref,
    w, ow, ck, cv, fill, gath, zsend, compact, scaled, gain, acc,
    sq_own, sq_peer, inv, kv_own, kv_send, kv_recv, q_send, q_recv, q_bf, kv_bf,
    ext, onehot, bias, scores, weights, o_own, o_peer, st_own, st_peer, att,
    hop_a, hop_b, got_a, got_b, out_l, out_r, fin_l, fin_r, hid,
    w_sem, in_sem, out_sem, xy_send, xy_recv, z_send, z_recv, x_send, x_recv,
    pr_send, pr_recv, o_send, o_recv, r_send, r_recv,
):
    row = lax.axis_index("row")
    col = lax.axis_index("col")
    vis = lax.axis_index("vis")
    z = lax.div(vis, YS)
    y = lax.rem(vis, YS)
    other = 1 - row
    right = lax.rem(col + 1, COLS)
    left = lax.rem(col + COLS - 1, COLS)
    across = lax.rem(col + 2, COLS)

    def at(r, c, v):
        return (r, c, v)

    block = y * COLS + col
    barrier = pltpu.get_barrier_semaphore()
    for step in range(1, 16):
        to = lax.rem(block + step, 16)
        pl.semaphore_signal(
            barrier, inc=1, device_id=at(row, lax.rem(to, COLS), z * YS + lax.div(to, COLS)), device_id_type=MESH)
    for step in range(1, ZS):
        pl.semaphore_signal(
            barrier, inc=1, device_id=at(row, col, lax.rem(z + step, ZS) * YS + y), device_id_type=MESH)
    pl.semaphore_signal(barrier, inc=1, device_id=at(other, col, vis), device_id_type=MESH)
    loads_w = []
    for j in (1, 2, 0):
        for part in range(4):
            rows = pl.ds(part * QUART, QUART)
            cp = pltpu.make_async_copy(w_hbm.at[j, rows], w.at[j, rows], w_sem.at[j * 4 + part])
            loads_w.append((j, cp))
    load_text = pltpu.make_async_copy(text_hbm, fill, in_sem.at[0])
    load_k = [pltpu.make_async_copy(ck_hbm.at[s], ck.at[s], in_sem.at[1 + s]) for s in range(REQS)]
    load_v = [pltpu.make_async_copy(cv_hbm.at[s], cv.at[s], in_sem.at[5 + s]) for s in range(REQS)]
    load_ow = [
        pltpu.make_async_copy(ow_hbm.at[pl.ds(p * 320, 320)], ow.at[pl.ds(p * 320, 320)], in_sem.at[9 + p])
        for p in range(4)
    ]
    own_rows = pl.ds(pl.multiple_of(block * 16, 16), 16)
    own_cols = pl.ds(pl.multiple_of(col * QUART, 128), QUART)
    load_own = pltpu.make_async_copy(image_hbm.at[:, own_cols], gath.at[own_rows], in_sem.at[13])
    load_own.start()
    load_text.start()

    pl.semaphore_wait(barrier, 23)
    for step in range(1, 16):
        to = lax.rem(block + step, 16)
        to_col = lax.rem(to, COLS)
        pltpu.make_async_remote_copy(
            src_ref=image_hbm.at[:, pl.ds(pl.multiple_of(to_col * QUART, 128), QUART)],
            dst_ref=gath.at[own_rows],
            send_sem=xy_send.at[step], recv_sem=xy_recv.at[step],
            device_id=at(row, to_col, z * YS + lax.div(to, COLS)), device_id_type=MESH).start()
    for _, cp in loads_w:
        cp.start()

    load_text.wait()
    for k in range(FEAT // HD):
        gain[:, k * HD:(k + 1) * HD] = jnp.broadcast_to(gain_ref[pl.ds(k * HD, HD)].reshape(1, HD), (8, HD))

    lane256 = lax.broadcasted_iota(jnp.int32, (128, TOK), 1)
    sub128 = lax.broadcasted_iota(jnp.int32, (128, TOK), 0)
    before = jnp.where(
        lax.broadcasted_iota(jnp.int32, (TOK, TOK), 0) < lax.broadcasted_iota(jnp.int32, (TOK, TOK), 1), 1.0, 0.0
    ).astype(BF16)
    to_rows = jnp.concatenate(
        [jnp.broadcast_to(slots_ref[pl.ds(zz * YS + y, 1), :], (16, TOK)) for zz in range(ZS)], axis=0)
    rank_of = sub128 & 3
    match = (to_rows >> 6) == (z * YS + ((sub128 & 15) >> 2))
    earlier = nn_dot(jnp.where(match, 1.0, 0.0).astype(BF16), before)
    chosen = match & (earlier.astype(jnp.int32) == rank_of)
    token_at = jnp.sum(
        jnp.where(chosen, (to_rows - z * TOK + 1).astype(F32), 0.0), axis=1, keepdims=True).astype(jnp.int32) - 1
    select = jnp.where(token_at == lane256, 1.0, 0.0).astype(BF16)

    here_rows = jnp.broadcast_to(slots_ref[pl.ds(vis, 1), :], (128, TOK))
    here = (here_rows >> 6) == (sub128 >> 2)
    here_before = nn_dot(jnp.where(here, 1.0, 0.0).astype(BF16), before)
    place_f = jnp.where(here & (here_before.astype(jnp.int32) == rank_of), 1.0, 0.0).T
    place = place_f.astype(BF16)
    has_image = jnp.sum(place_f, axis=1, keepdims=True)

    seg_rows = jnp.broadcast_to(seg_ref[...], (128, TOK))
    oh = jnp.where(seg_rows == sub128, 1.0, 0.0).T
    onehot[...] = oh.astype(BF16)
    lane128 = lax.broadcasted_iota(jnp.int32, (TOK, HALF), 1)
    tok128 = lax.broadcasted_iota(jnp.int32, (TOK, HALF), 0)
    seg_col = jnp.sum(oh * lane128.astype(F32), axis=1, keepdims=True).astype(jnp.int32)
    seg_mine = jnp.where(row == 0, seg_ref[:, :HALF], seg_ref[:, HALF:])
    bias[...] = jnp.where(
        (seg_col == seg_mine) & (lane128 + row * HALF <= tok128), 0.0, MASKED)
    for s in range(REQS):
        lane_c = lax.broadcasted_iota(jnp.int32, (CACHE, HD), 1)
        pos = lax.broadcasted_iota(jnp.int32, (CACHE, HD), 0) + row * CACHE
        seen = (lane_c == s) & (pos < lens_ref[0, s])
        ext[s] = jnp.where(seen | (lane_c >= REQS), 0.0, MASKED).astype(BF16)

    load_own.wait()
    for step in range(1, 16):
        frm = lax.rem(block + 16 - step, 16)
        rows = pl.ds(pl.multiple_of(frm * 16, 16), 16)
        pltpu.make_async_remote_copy(
            src_ref=gath.at[rows], dst_ref=gath.at[rows],
            send_sem=xy_send.at[step], recv_sem=xy_recv.at[step],
            device_id=at(row, col, vis), device_id_type=MESH).wait_recv()

    def block_at(dz, c_src):
        zz = lax.rem(z + dz, ZS)
        return compact.at[pl.ds(pl.multiple_of(zz * 16, 16), 16), pl.ds(pl.multiple_of(c_src * QUART, 128), QUART)]

    picked_rows = nn_dot(select, gath[...]).astype(BF16)
    zsend[...] = picked_rows
    for dz in Z_ORDER:
        zz = lax.rem(z + dz, ZS)
        pltpu.make_async_remote_copy(
            src_ref=zsend.at[pl.ds(pl.multiple_of(zz * 16, 16), 16)],
            dst_ref=block_at(0, col),
            send_sem=z_send.at[dz], recv_sem=z_recv.at[ZS - dz],
            device_id=at(row, col, zz * YS + y), device_id_type=MESH).start()
    block_own = pltpu.make_async_copy(
        zsend.at[pl.ds(pl.multiple_of(z * 16, 16), 16)], block_at(0, col), in_sem.at[14])
    block_own.start()
    for group in (load_k, load_v, load_ow):
        for cp in group:
            cp.start()

    def quarter(c_src):
        return pl.ds(pl.multiple_of(c_src * QUART, 128), QUART)

    def x_copy(c_src, to_col, lane):
        part = compact.at[:, quarter(c_src)]
        return pltpu.make_async_remote_copy(
            src_ref=part, dst_ref=part, send_sem=x_send.at[lane], recv_sem=x_recv.at[lane],
            device_id=at(row, to_col, vis), device_id_type=MESH)

    block_own.wait()
    for dz in Z_ORDER:
        pltpu.make_async_remote_copy(
            src_ref=block_at(dz, col), dst_ref=block_at(dz, col),
            send_sem=z_send.at[dz], recv_sem=z_recv.at[dz],
            device_id=at(row, col, vis), device_id_type=MESH).wait_recv()
    x_sends = [x_copy(col, right, 0), x_copy(col, left, 1), x_copy(col, across, 2)]
    for cp in x_sends[:2]:
        cp.start()

    def to_peer(src, dst, k):
        return pltpu.make_async_remote_copy(
            src_ref=src, dst_ref=dst, send_sem=pr_send.at[k], recv_sem=pr_recv.at[k],
            device_id=at(other, col, vis), device_id_type=MESH)

    def fill_quarter(c_src, squares):
        cols = quarter(c_src)
        rows_f = jnp.where(has_image > 0.0, nn_dot(place, compact[:, cols]), fill[:, cols].astype(F32))
        fill[:, cols] = rows_f.astype(BF16)
        scaled[:, cols] = (rows_f * gain[0:1, cols]).astype(BF16)
        for k in range(QUART // HD):
            piece = rows_f[:, k * HD:(k + 1) * HD]
            squares = squares + piece * piece
        return squares

    def product(c_src, j):
        return nn_dot(scaled[:, quarter(c_src)], w[j, quarter(c_src), :])

    def out_cols(j):
        return slice(j * WIDTH, (j + 1) * WIDTH)

    squares = fill_quarter(col, jnp.zeros((TOK, HD), F32))
    for jj, cp in loads_w:
        cp.wait()
    for j in range(3):
        acc[:, out_cols(j)] = product(col, j)
    for cp in x_sends[:2]:
        cp.wait_send()
    x_sends[2].start()
    for c_src, lane in ((left, 0), (right, 1)):
        x_copy(c_src, right, lane).wait_recv()
        squares = fill_quarter(c_src, squares)
    for j in range(3):
        acc[:, out_cols(j)] += product(left, j)
        acc[:, out_cols(j)] += product(right, j)
    x_copy(across, right, 2).wait_recv()
    squares = fill_quarter(across, squares)
    sq_own[...] = jnp.broadcast_to(jnp.sum(squares, axis=1, keepdims=True), (TOK, HD))
    sq_copy = to_peer(sq_own, sq_peer, 0)
    sq_copy.start()
    peer_copies = {0: to_peer(q_send, q_recv, 3)}
    acc[:, out_cols(0)] += product(across, 0)
    q_send[...] = acc[:, out_cols(0)].astype(BF16)
    peer_copies[0].start()
    my_rows = pl.ds(pl.multiple_of(row * HALF, HALF), HALF)
    its_rows = pl.ds(pl.multiple_of(other * HALF, HALF), HALF)
    for j in (1, 2):
        acc[:, out_cols(j)] += product(across, j)
        kv_send[j - 1] = acc[its_rows, out_cols(j)].astype(BF16)
        peer_copies[j] = to_peer(kv_send.at[j - 1], kv_recv.at[j - 1], j)
        peer_copies[j].start()

    sq_copy.wait()
    total_sq = sq_own[...] + sq_peer[...]
    inv[...] = lax.rsqrt(total_sq / D + EPSILON)
    per_request = jnp.sum(oh * total_sq, axis=0, keepdims=True)
    counts = jnp.sum(oh, axis=0, keepdims=True)
    rms_ref[...] = jnp.sqrt(per_request / (counts * D))[:, :REQS]
    inv_mine = inv[my_rows, :]
    outs = []
    peer_copies[0].wait()
    for h in range(HEADS_HERE):
        lanes = slice(h * HD, (h + 1) * HD)
        q_bf[:, lanes] = ((acc[:, lanes] + q_recv[:, lanes].astype(F32)) * inv[...]).astype(BF16)

    def finish_new(j, dst):
        peer_copies[j].wait()
        for h in range(HEADS_HERE):
            lanes = slice(h * HD, (h + 1) * HD)
            value = (acc[my_rows, j * WIDTH + h * HD:j * WIDTH + (h + 1) * HD] + kv_recv[j - 1, :, lanes].astype(F32)) * inv_mine
            kv_own[j - 1, :, lanes] = value
            kv_bf[j - 1, :, lanes] = value.astype(BF16)
        cp = pltpu.make_async_copy(kv_own.at[j - 1], dst, out_sem.at[j])
        cp.start()
        outs.append(cp)

    finish_new(1, nk_hbm)

    for group in (load_k, load_v):
        for cp in group:
            cp.wait()
    st_own[...] = jnp.zeros((TOK, HD), F32)

    def o_copy(h):
        lanes = pl.ds(pl.multiple_of(h * HD, HD), HD)
        return pltpu.make_async_remote_copy(
            src_ref=o_own.at[:, lanes], dst_ref=o_peer.at[:, lanes],
            send_sem=o_send.at[h], recv_sem=o_recv.at[h],
            device_id=at(other, col, vis), device_id_type=MESH)

    def weigh(h):
        lanes = pl.ds(pl.multiple_of(h * HD, HD), HD)
        q = q_bf[:, lanes]
        q_ext = jnp.concatenate([q, onehot[...]], axis=1)
        peak = nt_dot(q, kv_bf[0, :, lanes]) + bias[...]
        scores[:, REQS * CACHE:] = peak
        for s in range(REQS):
            part = nt_dot(q_ext, jnp.concatenate([ck[s, :, lanes], ext[s]], axis=1))
            scores[:, s * CACHE:(s + 1) * CACHE] = part
            for k in range(CACHE // HD):
                peak = jnp.maximum(peak, part[:, k * HD:(k + 1) * HD])
        top = jnp.max(peak, axis=1, keepdims=True) * SCALE_LOG2E
        weights[...] = jnp.exp2(scores[...] * SCALE_LOG2E - top).astype(BF16)
        return top

    def gather_values(h, top):
        lanes = pl.ds(pl.multiple_of(h * HD, HD), HD)
        ones = jnp.ones((CACHE, HD), BF16)
        total_acc = nn_dot(
            weights[:, REQS * CACHE:], jnp.concatenate([kv_bf[1, :, lanes], ones[:HALF]], axis=1))
        for s in range(REQS):
            total_acc = total_acc + nn_dot(
                weights[:, s * CACHE:(s + 1) * CACHE], jnp.concatenate([cv[s, :, lanes], ones], axis=1))
        total = total_acc[:, HD:]
        o_own[:, lanes] = (total_acc[:, :HD] / total).astype(BF16)
        st_own[...] = jnp.where(lane128 == h, top + jnp.log2(total), st_own[...])

    top = weigh(0)
    finish_new(2, nv_hbm)

    def head(h, top):
        gather_values(h, top)
        top = weigh(h + 1)
        o_copy(h).start()
        return top

    top = lax.fori_loop(0, HEADS_HERE - 1, head, top)
    gather_values(HEADS_HERE - 1, top)
    o_copy(HEADS_HERE - 1).start()
    st_copy = to_peer(st_own, st_peer, 4)
    st_copy.start()
    st_copy.wait()
    lead = st_own[...] - st_peer[...]
    mine = 1.0 / (1.0 + jnp.exp2(-lead))
    theirs = 1.0 / (1.0 + jnp.exp2(lead))
    for h in range(HEADS_HERE):
        lanes = slice(h * HD, (h + 1) * HD)
        o_copy(h).wait()
        att[:, lanes] = (
            o_own[:, lanes].astype(F32) * mine[:, h:h + 1] + o_peer[:, lanes].astype(F32) * theirs[:, h:h + 1]
        ).astype(BF16)

    for cp in load_ow:
        cp.wait()

    def share(c):
        return pl.ds(pl.multiple_of(c * SHARE, SHARE), SHARE)

    def ring(src, dst, k, lane, to_col):
        return pltpu.make_async_remote_copy(
            src_ref=src, dst_ref=dst, send_sem=r_send.at[k, lane], recv_sem=r_recv.at[k, lane],
            device_id=at(row, to_col, vis), device_id_type=MESH)

    def hop(n):
        return (
            ring(hop_a.at[n], got_a.at[n], n, 0, right),
            ring(hop_b.at[n], got_b.at[n], n, 1, left),
        )

    def last(n):
        return (
            ring(out_r.at[n], fin_l.at[n], n, 2, right),
            ring(out_l.at[n], fin_r.at[n], n, 3, left),
        )

    half = TILE // 2

    def second(n):
        one, two = hop(n)
        cols = pl.ds(n * TILE, TILE)
        one.wait_recv()
        two.wait_recv()
        to_right = acc[share(right), cols]
        out_r[n] = jnp.concatenate(
            [to_right[:, :half] + got_a[n].astype(F32), to_right[:, half:]], axis=1).astype(BF16)
        to_left = acc[share(left), cols]
        out_l[n] = jnp.concatenate(
            [to_left[:, :half], to_left[:, half:] + got_b[n].astype(F32)], axis=1).astype(BF16)
        for cp in last(n):
            cp.start()

    for n in range(TILES):
        cols = pl.ds(n * TILE, TILE)
        acc[:, cols] = nn_dot(att[...], ow[:, cols])
        far = acc[share(across), cols]
        hop_a[n] = far[:, :half].astype(BF16)
        hop_b[n] = far[:, half:].astype(BF16)
        for cp in hop(n):
            cp.start()
        if n >= 1:
            second(n - 1)
    second(TILES - 1)
    for n in range(TILES):
        cols = pl.ds(n * TILE, TILE)
        for cp in last(n):
            cp.wait_recv()
        hid[:, cols] = (
            fill[share(col), cols].astype(F32) + acc[share(col), cols]
            + (fin_l[n].astype(F32) + fin_r[n].astype(F32)))
        cp = pltpu.make_async_copy(hid.at[:, cols], hid_hbm.at[:, cols], out_sem.at[3 + n])
        cp.start()
        outs.append(cp)

    for step in range(1, 16):
        pltpu.make_async_remote_copy(
            src_ref=image_hbm.at[:, own_cols], dst_ref=gath.at[own_rows],
            send_sem=xy_send.at[step], recv_sem=xy_recv.at[step],
            device_id=at(other, col, vis), device_id_type=MESH).wait_send()
    for dz in Z_ORDER:
        pltpu.make_async_remote_copy(
            src_ref=zsend.at[pl.ds(0, 16)], dst_ref=block_at(0, col),
            send_sem=z_send.at[dz], recv_sem=z_recv.at[dz],
            device_id=at(other, col, vis), device_id_type=MESH).wait_send()
    x_sends[2].wait_send()
    for n in range(TILES):
        for cp in hop(n) + last(n):
            cp.wait_send()
    for cp in outs:
        cp.wait()


def hand_over(*refs):
    ins, outs, held, sems = refs[:4], refs[4:8], refs[8:11], refs[11]
    chunks = []
    for i in range(3):
        rows = ins[i].shape[0] // 2
        for k in range(2):
            part = pl.ds(k * rows, rows)
            chunks.append((
                pltpu.make_async_copy(ins[i].at[part], held[i].at[part], sems.at[0, 2 * i + k]),
                pltpu.make_async_copy(held[i].at[part], outs[i].at[part], sems.at[1, 2 * i + k]),
            ))
    for one, _ in chunks:
        one.start()
    outs[3][...] = ins[3][...]
    for one, two in chunks:
        one.wait()
        two.start()
    for _, two in chunks:
        two.wait()


def per_device(
    text_embed, image_embed, slot_source, segment_ids, prefix_lengths,
    attn_gain, qkv_weight, out_weight, cache_keys, cache_values,
):
    hbm = pl.BlockSpec(memory_space=pl.ANY)
    vmem = pl.BlockSpec(memory_space=pltpu.VMEM)
    smem = pl.BlockSpec(memory_space=pltpu.SMEM)

    def v(shape, dtype):
        return pltpu.VMEM(shape, dtype)

    dma = pltpu.SemaphoreType.DMA
    results = (
        jax.ShapeDtypeStruct((SHARE, FEAT), F32),
        jax.ShapeDtypeStruct((HALF, WIDTH), F32),
        jax.ShapeDtypeStruct((HALF, WIDTH), F32),
        jax.ShapeDtypeStruct((1, REQS), F32),
    )
    made = pl.pallas_call(
        kernel,
        out_shape=results,
        in_specs=[hbm, hbm, vmem, vmem, smem, vmem, hbm, hbm, hbm, hbm],
        out_specs=(hbm, hbm, hbm, vmem),
        scratch_shapes=[
            v((3, FEAT, WIDTH), BF16), v((WIDTH, FEAT), BF16),
            v((REQS, CACHE, WIDTH), BF16), v((REQS, CACHE, WIDTH), BF16),
            v((TOK, FEAT), BF16), v((TOK, QUART), BF16), v((HALF, QUART), BF16), v((HALF, FEAT), BF16),
            v((TOK, FEAT), BF16), v((8, FEAT), F32), v((TOK, 3 * WIDTH), F32),
            v((TOK, HD), F32), v((TOK, HD), F32), v((TOK, HD), F32),
            v((2, HALF, WIDTH), F32), v((2, HALF, WIDTH), BF16), v((2, HALF, WIDTH), BF16),
            v((TOK, WIDTH), BF16), v((TOK, WIDTH), BF16), v((TOK, WIDTH), BF16),
            v((2, HALF, WIDTH), BF16),
            v((REQS, CACHE, HD), BF16), v((TOK, HD), BF16), v((TOK, HALF), F32),
            v((TOK, REQS * CACHE + HALF), F32), v((TOK, REQS * CACHE + HALF), BF16),
            v((TOK, WIDTH), BF16), v((TOK, WIDTH), BF16), v((TOK, HD), F32), v((TOK, HD), F32),
            v((TOK, WIDTH), BF16),
            v((TILES, SHARE, TILE // 2), BF16), v((TILES, SHARE, TILE // 2), BF16),
            v((TILES, SHARE, TILE // 2), BF16), v((TILES, SHARE, TILE // 2), BF16),
            v((TILES, SHARE, TILE), BF16), v((TILES, SHARE, TILE), BF16),
            v((TILES, SHARE, TILE), BF16), v((TILES, SHARE, TILE), BF16),
            v((SHARE, FEAT), F32),
            dma((12,)), dma((15,)), dma((8,)), dma((16,)), dma((16,)), dma((8,)), dma((8,)),
            dma((3,)), dma((3,)), dma((5,)), dma((5,)), dma((HEADS_HERE,)), dma((HEADS_HERE,)),
            dma((TILES, 4)), dma((TILES, 4)),
        ],
        compiler_params=pltpu.CompilerParams(
            collective_id=0, has_side_effects=True, vmem_limit_bytes=60 * 1024 * 1024),
    )(
        text_embed[0], image_embed[0], slot_source, segment_ids, prefix_lengths,
        attn_gain, qkv_weight.transpose(1, 0, 2), out_weight, cache_keys[0], cache_values[0],
    )
    hidden, keys, values, rms = pl.pallas_call(
        hand_over,
        out_shape=results,
        in_specs=[hbm, hbm, hbm, vmem],
        out_specs=(hbm, hbm, hbm, vmem),
        scratch_shapes=[v((SHARE, FEAT), F32), v((HALF, WIDTH), F32), v((HALF, WIDTH), F32), dma((2, 6))],
    )(*made)
    return hidden[None], keys[None], values[None], rms


def solution(mesh):
    return jax.shard_map(
        per_device,
        mesh=mesh,
        in_specs=(
            P("vis", None, "row"),
            P("vis", "col", "row"),
            P(),
            P("vis", None),
            P("vis", None),
            P("row"),
            P("row", None, "col"),
            P("col", "row"),
            P("vis", None, "row", "col"),
            P("vis", None, "row", "col"),
        ),
        out_specs=(
            P("vis", "col", "row"),
            P("vis", "row", "col"),
            P("vis", "row", "col"),
            P("vis", None),
        ),
        check_vma=False,
    )
```

time: 94.5 us -> 77.3 us (0.82)
  the two profiles are of different devices: /device:TPU:2 before, /device:TPU:24 now
where the time goes in v2:
time: 77.3 us; the launch traced here: 77.1 us
  Pallas kernels  76.3 us (99%)
  between operations  0.8 us (1%)
    pallas_call x1, Pallas kernels, per_device(): pl.pallas_call(kernel, out_shape=results, in_specs=[hbm, hbm, vmem, vmem,...  72.8 us
    pallas_call x1, Pallas kernels, per_device(): pl.pallas_call(hand_over, out_shape=results, in_specs=[hbm, hbm, hbm, vme...  3.49 us

profile of v2, /device:TPU:24, one launch (start us, length us, event | category | flops | bytes accessed | tf_op | source)
XLA Modules:
  0.0 77.1 jit_solution(8513568549814811658)
XLA Ops:
  0.6 72.8 %shard_map.129 = (f32[64,2560]{1,0:T(8,128)}, f32[128,1280]{1,0:T(8,128)}, f32[128,1280]{1,0:T(8,128)}, f32[1,4]{1,0:T(1,128)}) custom-call(bf16[256,2560]{1,0:T(8,128)(2,1)} %bitcast.11, bf16[16,2560]{1,0:T(8,128)(2,1)} %bitcast.12, s32[32,256]{1,0:T(8,128)} %slots_ref.1, s32[1,256]{1,0:T(1,128)} %seg_ref.1, s32[1,4]{1,0:T(1,128)} %lens_ref.1, ...), custom_call_target="tpu_custom_call" | custom-call | tf_op jit(solution)/shard_map/pallas_call | solution.py:458
  73.4 3.5 %shard_map.130 = (f32[64,2560]{1,0:T(8,128)}, f32[128,1280]{1,0:T(8,128)}, f32[128,1280]{1,0:T(8,128)}, f32[1,4]{1,0:T(1,128)}) custom-call(f32[64,2560]{1,0:T(8,128)} %get-tuple-element.12.refs_0_, f32[128,1280]{1,0:T(8,128)} %get-tuple-element.13.refs_1_, f32[128,1280]{1,0:T(8,128)} %get-tuple-element.14.refs_2_, f32[1,4]{1,0:T(1,128)} %get-tuple-element.15.refs_3_), custom_call_target="tpu_custom_call" | custom-call | tf_op jit(solution)/shard_map/pallas_call | solution.py:491

commit v3 on v2

v3 whole, which is shorter than its diff:
```python
import functools

import jax
import jax.numpy as jnp
from jax import lax
from jax.experimental import pallas as pl
from jax.experimental.pallas import tpu as pltpu
from jax.sharding import PartitionSpec as P

D = 5120
HD = 128
EPSILON = 1e-06
MASKED = -1e30
SCALE_LOG2E = HD ** (-0.5) * 1.4426950408889634

MESH = pl.DeviceIdType.MESH
F32 = jnp.float32
BF16 = jnp.bfloat16

COLS = 4
ZS = 8
YS = 4
TOK = 256
FEAT = 2560
QUART = 640
WIDTH = 1280
HEADS_HERE = 10
CACHE = 512
REQS = 4
HALF = 128
SHARE = 64
LOW = SHARE // 2
TILE = 1280
TILES = FEAT // TILE
Z_ORDER = (0, 1, 7, 2, 6, 3, 5, 4)


def nt_dot(left, right):
    return lax.dot_general(left, right, (((1,), (1,)), ((), ())), preferred_element_type=F32)


def nn_dot(left, right):
    return jnp.dot(left, right, preferred_element_type=F32)


def kernel(
    text_hbm, image_hbm, slots_ref, seg_ref, lens_ref, gain_ref, w_hbm, ow_hbm, ck_hbm, cv_hbm,
    hid_ref, nk_ref, nv_ref, rms_ref,
    w, ow, ck, cv, fill, gath, zsend, compact, scaled, gain, acc,
    sq_own, sq_peer, inv, kv_send, kv_recv, q_send, q_recv, q_bf, kv_bf,
    ext, onehot_t, bias_t, onehot, bias, scores, weights, o_own, o_peer, st_own, st_peer, att,
    to_across, to_right, to_left, from_across, from_left, from_right,
    w_sem, in_sem, xy_send, xy_recv, z_send, z_recv, x_send, x_recv,
    pr_send, pr_recv, o_send, o_recv, r_send, r_recv,
):
    row = lax.axis_index("row")
    col = lax.axis_index("col")
    vis = lax.axis_index("vis")
    z = lax.div(vis, YS)
    y = lax.rem(vis, YS)
    other = 1 - row
    right = lax.rem(col + 1, COLS)
    left = lax.rem(col + COLS - 1, COLS)
    across = lax.rem(col + 2, COLS)

    def at(r, c, v):
        return (r, c, v)

    block = y * COLS + col
    barrier = pltpu.get_barrier_semaphore()
    for step in (4, 3, 5, 2, 6, 1, 7):
        pl.semaphore_signal(
            barrier, inc=1, device_id=at(row, col, lax.rem(z + step, ZS) * YS + y), device_id_type=MESH)
    for step in range(1, 16):
        to = lax.rem(block + step, 16)
        pl.semaphore_signal(
            barrier, inc=1, device_id=at(row, lax.rem(to, COLS), z * YS + lax.div(to, COLS)), device_id_type=MESH)
    pl.semaphore_signal(barrier, inc=1, device_id=at(other, col, vis), device_id_type=MESH)
    loads_w = []
    for j in (1, 2, 0):
        for part in range(4):
            rows = pl.ds(part * QUART, QUART)
            cp = pltpu.make_async_copy(w_hbm.at[j, rows], w.at[j, rows], w_sem.at[j * 4 + part])
            loads_w.append((j, cp))
    load_text = pltpu.make_async_copy(text_hbm, fill, in_sem.at[0])
    load_k = [pltpu.make_async_copy(ck_hbm.at[s], ck.at[s], in_sem.at[1 + s]) for s in range(REQS)]
    load_v = [pltpu.make_async_copy(cv_hbm.at[s], cv.at[s], in_sem.at[5 + s]) for s in range(REQS)]
    load_ow = [
        pltpu.make_async_copy(ow_hbm.at[pl.ds(p * 320, 320)], ow.at[pl.ds(p * 320, 320)], in_sem.at[9 + p])
        for p in range(4)
    ]
    own_rows = pl.ds(pl.multiple_of(block * 16, 16), 16)
    own_cols = pl.ds(pl.multiple_of(col * QUART, 128), QUART)
    load_own = pltpu.make_async_copy(image_hbm.at[:, own_cols], gath.at[own_rows], in_sem.at[13])
    load_own.start()
    load_text.start()

    pl.semaphore_wait(barrier, 23)
    for step in range(1, 16):
        to = lax.rem(block + step, 16)
        to_col = lax.rem(to, COLS)
        pltpu.make_async_remote_copy(
            src_ref=image_hbm.at[:, pl.ds(pl.multiple_of(to_col * QUART, 128), QUART)],
            dst_ref=gath.at[own_rows],
            send_sem=xy_send.at[step], recv_sem=xy_recv.at[step],
            device_id=at(row, to_col, z * YS + lax.div(to, COLS)), device_id_type=MESH).start()
    for _, cp in loads_w:
        cp.start()

    load_text.wait()
    for k in range(FEAT // HD):
        gain[:, k * HD:(k + 1) * HD] = jnp.broadcast_to(gain_ref[pl.ds(k * HD, HD)].reshape(1, HD), (8, HD))

    lane256 = lax.broadcasted_iota(jnp.int32, (128, TOK), 1)
    sub128 = lax.broadcasted_iota(jnp.int32, (128, TOK), 0)
    before = jnp.where(
        lax.broadcasted_iota(jnp.int32, (TOK, TOK), 0) < lax.broadcasted_iota(jnp.int32, (TOK, TOK), 1), 1.0, 0.0
    ).astype(BF16)
    to_rows = jnp.concatenate(
        [jnp.broadcast_to(slots_ref[pl.ds(zz * YS + y, 1), :], (16, TOK)) for zz in range(ZS)], axis=0)
    rank_of = sub128 & 3
    match = (to_rows >> 6) == (z * YS + ((sub128 & 15) >> 2))
    earlier = nn_dot(jnp.where(match, 1.0, 0.0).astype(BF16), before)
    chosen = match & (earlier.astype(jnp.int32) == rank_of)
    token_at = jnp.sum(
        jnp.where(chosen, (to_rows - z * TOK + 1).astype(F32), 0.0), axis=1, keepdims=True).astype(jnp.int32) - 1
    select = jnp.where(token_at == lane256, 1.0, 0.0).astype(BF16)

    here_rows = jnp.broadcast_to(slots_ref[pl.ds(vis, 1), :], (128, TOK))
    slab = sub128 >> 4
    offset = jnp.zeros_like(slab)
    for i, dz in enumerate(Z_ORDER):
        offset = jnp.where(slab == i, dz, offset)
    here = (here_rows >> 6) == (((z + offset) & (ZS - 1)) * YS + ((sub128 & 15) >> 2))
    here_before = nn_dot(jnp.where(here, 1.0, 0.0).astype(BF16), before)
    place_f = jnp.where(here & (here_before.astype(jnp.int32) == rank_of), 1.0, 0.0).T
    place = place_f.astype(BF16)
    has_image = jnp.sum(place_f, axis=1, keepdims=True)

    seg_rows = jnp.broadcast_to(seg_ref[...], (128, TOK))
    oh = jnp.where(seg_rows == sub128, 1.0, 0.0).T
    onehot_t[...] = oh.astype(BF16)
    lane128 = lax.broadcasted_iota(jnp.int32, (TOK, HALF), 1)
    tok128 = lax.broadcasted_iota(jnp.int32, (TOK, HALF), 0)
    seg_col = jnp.sum(oh * lane128.astype(F32), axis=1, keepdims=True).astype(jnp.int32)
    seg_mine = jnp.where(row == 0, seg_ref[:, :HALF], seg_ref[:, HALF:])
    bias_t[...] = jnp.where(
        (seg_col == seg_mine) & (lane128 + row * HALF <= tok128), 0.0, MASKED)
    spans = (
        (across * SHARE, SHARE), (right * SHARE, LOW), (left * SHARE, LOW),
        (right * SHARE + LOW, LOW), (left * SHARE + LOW, LOW), (col * SHARE, SHARE),
    )
    moves = []
    for start, count in spans:
        first = sum(m[2] for m in moves)
        moves.append((pl.ds(pl.multiple_of(start, LOW), count), slice(first, first + count), count))
    for src, dst, _ in moves:
        onehot[dst, :] = onehot_t[src, :]
        bias[dst, :] = bias_t[src, :]
    for s in range(REQS):
        lane_c = lax.broadcasted_iota(jnp.int32, (CACHE, HD), 1)
        pos = lax.broadcasted_iota(jnp.int32, (CACHE, HD), 0) + row * CACHE
        seen = (lane_c == s) & (pos < lens_ref[0, s])
        ext[s] = jnp.where(seen | (lane_c >= REQS), 0.0, MASKED).astype(BF16)

    load_own.wait()
    for step in range(1, 16):
        frm = lax.rem(block + 16 - step, 16)
        rows = pl.ds(pl.multiple_of(frm * 16, 16), 16)
        pltpu.make_async_remote_copy(
            src_ref=gath.at[rows], dst_ref=gath.at[rows],
            send_sem=xy_send.at[step], recv_sem=xy_recv.at[step],
            device_id=at(row, col, vis), device_id_type=MESH).wait_recv()

    def block_at(dz):
        return compact.at[pl.ds(Z_ORDER.index(dz) * 16, 16), own_cols]

    picked_rows = nn_dot(select, gath[...]).astype(BF16)
    zsend[...] = picked_rows
    for dz in Z_ORDER[1:]:
        zz = lax.rem(z + dz, ZS)
        pltpu.make_async_remote_copy(
            src_ref=zsend.at[pl.ds(pl.multiple_of(zz * 16, 16), 16)],
            dst_ref=block_at(ZS - dz),
            send_sem=z_send.at[dz], recv_sem=z_recv.at[ZS - dz],
            device_id=at(row, col, zz * YS + y), device_id_type=MESH).start()
    block_own = pltpu.make_async_copy(
        zsend.at[pl.ds(pl.multiple_of(z * 16, 16), 16)], block_at(0), in_sem.at[14])
    block_own.start()
    for group in (load_k, load_v, load_ow):
        for cp in group:
            cp.start()

    def quarter(c_src):
        return pl.ds(pl.multiple_of(c_src * QUART, 128), QUART)

    def x_copy(c_src, to_col, lane):
        rows = pl.ds(0, 128) if lane == 4 else pl.ds(lane % 2 * 64, 64)
        part = compact.at[rows, quarter(c_src)]
        return pltpu.make_async_remote_copy(
            src_ref=part, dst_ref=part, send_sem=x_send.at[lane], recv_sem=x_recv.at[lane],
            device_id=at(row, to_col, vis), device_id_type=MESH)

    x_sends = [x_copy(col, right if lane < 2 else left, lane) for lane in range(4)] + [x_copy(col, across, 4)]
    block_own.wait()
    for i, dz in enumerate(Z_ORDER):
        if i > 0:
            pltpu.make_async_remote_copy(
                src_ref=block_at(dz), dst_ref=block_at(dz),
                send_sem=z_send.at[dz], recv_sem=z_recv.at[dz],
                device_id=at(row, col, vis), device_id_type=MESH).wait_recv()
        if i == 3:
            x_sends[0].start()
            x_sends[2].start()
    x_sends[1].start()
    x_sends[3].start()

    def to_peer(src, dst, k):
        return pltpu.make_async_remote_copy(
            src_ref=src, dst_ref=dst, send_sem=pr_send.at[k], recv_sem=pr_recv.at[k],
            device_id=at(other, col, vis), device_id_type=MESH)

    def fill_quarter(c_src, squares):
        cols = quarter(c_src)
        rows_f = jnp.where(has_image > 0.0, nn_dot(place, compact[:, cols]), fill[:, cols].astype(F32))
        fill[:, cols] = rows_f.astype(BF16)
        scaled[:, cols] = (rows_f * gain[0:1, cols]).astype(BF16)
        for k in range(QUART // HD):
            piece = rows_f[:, k * HD:(k + 1) * HD]
            squares = squares + piece * piece
        return squares

    def product(c_src, j):
        return nn_dot(scaled[:, quarter(c_src)], w[j, quarter(c_src), :])

    def out_cols(j):
        return slice(j * WIDTH, (j + 1) * WIDTH)

    squares = fill_quarter(col, jnp.zeros((TOK, HD), F32))
    for jj, cp in loads_w:
        cp.wait()
    for j in range(3):
        acc[:, out_cols(j)] = product(col, j)
    for cp in x_sends[:4]:
        cp.wait_send()
    x_sends[4].start()
    for c_src, lane in ((left, 0), (right, 2)):
        x_copy(c_src, across, lane).wait_recv()
        x_copy(c_src, across, lane + 1).wait_recv()
        squares = fill_quarter(c_src, squares)
    for j in range(3):
        acc[:, out_cols(j)] += product(left, j)
        acc[:, out_cols(j)] += product(right, j)
    x_copy(across, right, 4).wait_recv()
    squares = fill_quarter(across, squares)
    sq_own[...] = jnp.broadcast_to(jnp.sum(squares, axis=1, keepdims=True), (TOK, HD))
    sq_copy = to_peer(sq_own, sq_peer, 0)
    sq_copy.start()
    peer_copies = {0: to_peer(q_send, q_recv, 3)}
    acc[:, out_cols(0)] += product(across, 0)
    q_send[...] = acc[:, out_cols(0)].astype(BF16)
    peer_copies[0].start()
    my_rows = pl.ds(pl.multiple_of(row * HALF, HALF), HALF)
    its_rows = pl.ds(pl.multiple_of(other * HALF, HALF), HALF)
    for j in (1, 2):
        acc[:, out_cols(j)] += product(across, j)
        kv_send[j - 1] = acc[its_rows, out_cols(j)].astype(BF16)
        peer_copies[j] = to_peer(kv_send.at[j - 1], kv_recv.at[j - 1], j)
        peer_copies[j].start()

    sq_copy.wait()
    total_sq = sq_own[...] + sq_peer[...]
    inv[...] = lax.rsqrt(total_sq / D + EPSILON)
    per_request = jnp.sum(oh * total_sq, axis=0, keepdims=True)
    counts = jnp.sum(oh, axis=0, keepdims=True)
    rms_ref[...] = jnp.sqrt(per_request / (counts * D))[:, :REQS]
    inv_mine = inv[my_rows, :]
    peer_copies[0].wait()
    for src, dst, _ in moves:
        inv_rows = inv[src, :]
        for h in range(HEADS_HERE):
            lanes = slice(h * HD, (h + 1) * HD)
            q_bf[dst, lanes] = ((acc[src, lanes] + q_recv[src, lanes].astype(F32)) * inv_rows).astype(BF16)

    def finish_new(j, dst):
        peer_copies[j].wait()
        for h in range(HEADS_HERE):
            lanes = slice(h * HD, (h + 1) * HD)
            value = (acc[my_rows, j * WIDTH + h * HD:j * WIDTH + (h + 1) * HD] + kv_recv[j - 1, :, lanes].astype(F32)) * inv_mine
            dst[:, lanes] = value
            kv_bf[j - 1, :, lanes] = value.astype(BF16)

    finish_new(1, nk_ref)

    for group in (load_k, load_v):
        for cp in group:
            cp.wait()
    st_own[...] = jnp.zeros((TOK, HD), F32)

    def rows_of(part):
        return slice(part * HALF, (part + 1) * HALF)

    def o_copy(part, h):
        where = (pl.ds(part * HALF, HALF), pl.ds(pl.multiple_of(h * HD, HD), HD))
        return pltpu.make_async_remote_copy(
            src_ref=o_own.at[where], dst_ref=o_peer.at[where],
            send_sem=o_send.at[part, h], recv_sem=o_recv.at[part, h],
            device_id=at(other, col, vis), device_id_type=MESH)

    def st_copy(part):
        where = pl.ds(part * HALF, HALF)
        return to_peer(st_own.at[where], st_peer.at[where], 4 + part)

    def weigh(part, h):
        lanes = pl.ds(pl.multiple_of(h * HD, HD), HD)
        q = q_bf[rows_of(part), lanes]
        q_ext = jnp.concatenate([q, onehot[rows_of(part), :]], axis=1)
        peak = nt_dot(q, kv_bf[0, :, lanes]) + bias[rows_of(part), :]
        scores[:, REQS * CACHE:] = peak
        for s in range(REQS):
            piece = nt_dot(q_ext, jnp.concatenate([ck[s, :, lanes], ext[s]], axis=1))
            scores[:, s * CACHE:(s + 1) * CACHE] = piece
            for k in range(CACHE // HD):
                peak = jnp.maximum(peak, piece[:, k * HD:(k + 1) * HD])
        top = jnp.max(peak, axis=1, keepdims=True) * SCALE_LOG2E
        weights[...] = jnp.exp2(scores[...] * SCALE_LOG2E - top).astype(BF16)
        return top

    lane_h = lax.broadcasted_iota(jnp.int32, (HALF, HD), 1)

    def gather_values(part, h, top):
        lanes = pl.ds(pl.multiple_of(h * HD, HD), HD)
        ones = jnp.ones((CACHE, HD), BF16)
        total_acc = nn_dot(
            weights[:, REQS * CACHE:], jnp.concatenate([kv_bf[1, :, lanes], ones[:HALF]], axis=1))
        for s in range(REQS):
            total_acc = total_acc + nn_dot(
                weights[:, s * CACHE:(s + 1) * CACHE], jnp.concatenate([cv[s, :, lanes], ones], axis=1))
        total = total_acc[:, HD:]
        o_own[rows_of(part), lanes] = (total_acc[:, :HD] / total).astype(BF16)
        st_own[rows_of(part), :] = jnp.where(lane_h == h, top + jnp.log2(total), st_own[rows_of(part), :])

    def all_heads(part, top):
        def head(h, top):
            gather_values(part, h, top)
            top = weigh(part, h + 1)
            o_copy(part, h).start()
            return top

        top = lax.fori_loop(0, HEADS_HERE - 1, head, top)
        gather_values(part, HEADS_HERE - 1, top)
        o_copy(part, HEADS_HERE - 1).start()
        st_copy(part).start()

    def join(part):
        st_copy(part).wait()
        lead = st_own[rows_of(part), :] - st_peer[rows_of(part), :]
        mine = 1.0 / (1.0 + jnp.exp2(-lead))
        theirs = 1.0 / (1.0 + jnp.exp2(lead))
        for h in range(HEADS_HERE):
            lanes = slice(h * HD, (h + 1) * HD)
            o_copy(part, h).wait()
            att[:, lanes] = (
                o_own[rows_of(part), lanes].astype(F32) * mine[:, h:h + 1]
                + o_peer[rows_of(part), lanes].astype(F32) * theirs[:, h:h + 1]
            ).astype(BF16)

    low, high = pl.ds(0, LOW), pl.ds(LOW, LOW)

    def ring(n, lane):
        src, dst, to_col = (
            (to_across.at[n], from_across.at[n], across),
            (to_right.at[n, low], from_left.at[n, low], right),
            (to_left.at[n, low], from_right.at[n, low], left),
            (to_right.at[n, high], from_left.at[n, high], right),
            (to_left.at[n, high], from_right.at[n, high], left),
        )[lane]
        return pltpu.make_async_remote_copy(
            src_ref=src, dst_ref=dst, send_sem=r_send.at[n, lane], recv_sem=r_recv.at[n, lane],
            device_id=at(row, to_col, vis), device_id_type=MESH)

    top = weigh(0, 0)
    finish_new(2, nv_ref)
    all_heads(0, top)
    top = weigh(1, 0)
    join(0)
    for cp in load_ow:
        cp.wait()
    for n in range(TILES):
        piece = nn_dot(att[...], ow[:, n * TILE:(n + 1) * TILE])
        to_across[n] = piece[:SHARE].astype(BF16)
        ring(n, 0).start()
        to_right[n, :LOW] = piece[SHARE:SHARE + LOW].astype(BF16)
        to_left[n, :LOW] = piece[SHARE + LOW:].astype(BF16)
        ring(n, 1).start()
        ring(n, 2).start()
    all_heads(1, top)
    join(1)
    for n in range(TILES):
        piece = nn_dot(att[...], ow[:, n * TILE:(n + 1) * TILE])
        to_right[n, LOW:] = piece[:LOW].astype(BF16)
        to_left[n, LOW:] = piece[LOW:SHARE].astype(BF16)
        ring(n, 3).start()
        ring(n, 4).start()
        acc[:SHARE, n * TILE:(n + 1) * TILE] = piece[SHARE:]
    own_share = pl.ds(pl.multiple_of(col * SHARE, SHARE), SHARE)
    for n in range(TILES):
        cols = slice(n * TILE, (n + 1) * TILE)
        for lane in range(5):
            ring(n, lane).wait_recv()
        hid_ref[:, cols] = (
            fill[own_share, cols].astype(F32) + acc[:SHARE, cols] + from_across[n].astype(F32)
            + (from_left[n].astype(F32) + from_right[n].astype(F32)))

    for step in range(1, 16):
        pltpu.make_async_remote_copy(
            src_ref=image_hbm.at[:, own_cols], dst_ref=gath.at[own_rows],
            send_sem=xy_send.at[step], recv_sem=xy_recv.at[step],
            device_id=at(other, col, vis), device_id_type=MESH).wait_send()
    for dz in Z_ORDER[1:]:
        pltpu.make_async_remote_copy(
            src_ref=zsend.at[pl.ds(0, 16)], dst_ref=block_at(0),
            send_sem=z_send.at[dz], recv_sem=z_recv.at[dz],
            device_id=at(other, col, vis), device_id_type=MESH).wait_send()
    x_sends[4].wait_send()
    for n in range(TILES):
        for lane in range(5):
            ring(n, lane).wait_send()


def per_device(
    text_embed, image_embed, slot_source, segment_ids, prefix_lengths,
    attn_gain, qkv_weight, out_weight, cache_keys, cache_values,
):
    hbm = pl.BlockSpec(memory_space=pl.ANY)
    vmem = pl.BlockSpec(memory_space=pltpu.VMEM)
    smem = pl.BlockSpec(memory_space=pltpu.SMEM)

    def v(shape, dtype):
        return pltpu.VMEM(shape, dtype)

    dma = pltpu.SemaphoreType.DMA
    results = (
        jax.ShapeDtypeStruct((SHARE, FEAT), F32),
        jax.ShapeDtypeStruct((HALF, WIDTH), F32),
        jax.ShapeDtypeStruct((HALF, WIDTH), F32),
        jax.ShapeDtypeStruct((1, REQS), F32),
    )
    made = pl.pallas_call(
        kernel,
        out_shape=tuple(v(r.shape, r.dtype) for r in results),
        in_specs=[hbm, hbm, vmem, vmem, smem, vmem, hbm, hbm, hbm, hbm],
        out_specs=(vmem, vmem, vmem, vmem),
        scratch_shapes=[
            v((3, FEAT, WIDTH), BF16), v((WIDTH, FEAT), BF16),
            v((REQS, CACHE, WIDTH), BF16), v((REQS, CACHE, WIDTH), BF16),
            v((TOK, FEAT), BF16), v((TOK, QUART), BF16), v((HALF, QUART), BF16), v((HALF, FEAT), BF16),
            v((TOK, FEAT), BF16), v((8, FEAT), F32), v((TOK, 3 * WIDTH), F32),
            v((TOK, HD), F32), v((TOK, HD), F32), v((TOK, HD), F32),
            v((2, HALF, WIDTH), BF16), v((2, HALF, WIDTH), BF16),
            v((TOK, WIDTH), BF16), v((TOK, WIDTH), BF16), v((TOK, WIDTH), BF16),
            v((2, HALF, WIDTH), BF16),
            v((REQS, CACHE, HD), BF16), v((TOK, HD), BF16), v((TOK, HALF), F32),
            v((TOK, HD), BF16), v((TOK, HALF), F32),
            v((HALF, REQS * CACHE + HALF), F32), v((HALF, REQS * CACHE + HALF), BF16),
            v((TOK, WIDTH), BF16), v((TOK, WIDTH), BF16), v((TOK, HD), F32), v((TOK, HD), F32),
            v((HALF, WIDTH), BF16),
            v((TILES, SHARE, TILE), BF16), v((TILES, SHARE, TILE), BF16), v((TILES, SHARE, TILE), BF16),
            v((TILES, SHARE, TILE), BF16), v((TILES, SHARE, TILE), BF16), v((TILES, SHARE, TILE), BF16),
            dma((12,)), dma((15,)), dma((16,)), dma((16,)), dma((8,)), dma((8,)),
            dma((5,)), dma((5,)), dma((6,)), dma((6,)), dma((2, HEADS_HERE)), dma((2, HEADS_HERE)),
            dma((TILES, 5)), dma((TILES, 5)),
        ],
        compiler_params=pltpu.CompilerParams(
            collective_id=0, has_side_effects=True, vmem_limit_bytes=60 * 1024 * 1024),
    )(
        text_embed[0], image_embed[0], slot_source, segment_ids, prefix_lengths,
        attn_gain, qkv_weight.transpose(1, 0, 2), out_weight, cache_keys[0], cache_values[0],
    )
    hidden, keys, values, rms = made
    return hidden[None], keys[None], values[None], rms


def solution(mesh):
    return jax.shard_map(
        per_device,
        mesh=mesh,
        in_specs=(
            P("vis", None, "row"),
            P("vis", "col", "row"),
            P(),
            P("vis", None),
            P("vis", None),
            P("row"),
            P("row", None, "col"),
            P("col", "row"),
            P("vis", None, "row", "col"),
            P("vis", None, "row", "col"),
        ),
        out_specs=(
            P("vis", "col", "row"),
            P("vis", "row", "col"),
            P("vis", "row", "col"),
            P("vis", None),
        ),
        check_vma=False,
    )
```

time: 77.3 us -> 70.4 us (0.911)
  the two profiles are of different devices: /device:TPU:24 before, /device:TPU:2 now
where the time goes in v3:
time: 70.4 us; the launch traced here: 69.5 us
  Pallas kernels  65.9 us (94%)
  local copies, waits for them, and re-layouts  3.02 us (4%)
    pallas_call x1, Pallas kernels, per_device(): pl.pallas_call(kernel, out_shape=tuple((v(r.shape, r.dtype) for r in resu...  65.9 us
    unnamed x4, local copies, waits for them, and re-layouts  3.02 us

profile of v3, /device:TPU:2, one launch (start us, length us, event | category | flops | bytes accessed | tf_op | source)
XLA Modules:
  0.0 69.5 jit_solution(14759242773835086443)
XLA Ops:
  0.6 65.9 %shard_map.129 = (f32[64,2560]{1,0:T(8,128)S(1)}, f32[128,1280]{1,0:T(8,128)S(1)}, f32[128,1280]{1,0:T(8,128)S(1)}, f32[1,4]{1,0:T(1,128)S(1)}) custom-call(bf16[256,2560]{1,0:T(8,128)(2,1)} %bitcast.14, bf16[16,2560]{1,0:T(8,128)(2,1)} %bitcast.15, s32[32,256]{1,0:T(8,128)} %slots_ref.1, s32[1,256]{1,0:T(1,128)} %seg_ref.1, s32[1,4]{1,0:T(1,128)} %lens_ref.1, ...), custom_call_target="tpu_custom_call" | custom-call | tf_op jit(solution)/shard_map/pallas_call | solution.py:449
  66.5 0.8 %copy.18 = f32[1,64,2560]{2,1,0:T(8,128)} copy(f32[1,64,2560]{2,1,0:T(8,128)S(1)} %bitcast.10) | data formatting | bytes 1310720
  67.4 0.8 %copy.19 = f32[1,128,1280]{2,1,0:T(8,128)} copy(f32[1,128,1280]{2,1,0:T(8,128)S(1)} %bitcast.9) | data formatting | bytes 1310720
  68.2 0.5 copy.21
  68.7 0.8 %copy.20 = f32[1,128,1280]{2,1,0:T(8,128)} copy(f32[1,128,1280]{2,1,0:T(8,128)S(1)} %bitcast.8) | data formatting | bytes 1310720

commit v4 on v3

--- a/solution.py
+++ b/solution.py
@@ -426,6 +426,15 @@
     for n in range(TILES):
         for lane in range(5):
             ring(n, lane).wait_send()
+
+
+def hand_over(*refs):
+    ins, outs, sems = refs[:4], refs[4:8], refs[8]
+    copies = [pltpu.make_async_copy(ins[i], outs[i], sems.at[i]) for i in range(4)]
+    for cp in copies:
+        cp.start()
+    for cp in copies:
+        cp.wait()
 
 
 def per_device(
@@ -477,7 +486,14 @@
         text_embed[0], image_embed[0], slot_source, segment_ids, prefix_lengths,
         attn_gain, qkv_weight.transpose(1, 0, 2), out_weight, cache_keys[0], cache_values[0],
     )
-    hidden, keys, values, rms = made
+    hidden, keys, values, rms = pl.pallas_call(
+        hand_over,
+        out_shape=results,
+        in_specs=[hbm, hbm, hbm, hbm],
+        out_specs=(hbm, hbm, hbm, hbm),
+        scratch_shapes=[dma((4,))],
+        compiler_params=pltpu.CompilerParams(vmem_limit_bytes=1024 * 1024),
+    )(*made)
     return hidden[None], keys[None], values[None], rms
 
 

time: 70.4 us -> 68.7 us (0.976)
  local copies, waits for them, and re-layouts: 3.02 us -> 0 us
  Pallas kernels: 65.9 us -> 67.2 us
    unnamed x4 -> x0, local copies, waits for them, and re-layouts: 3.02 us -> none
    pallas_call x0 -> x1, Pallas kernels: none -> 1.31 us  [per_device(): pl.pallas_call(hand_over, out_shape=results, in_specs=[hbm, hbm, hbm, hbm...]
where the time goes in v4:
time: 68.7 us; the launch traced here: 67.8 us
  Pallas kernels  67.2 us (98%)
    pallas_call x1, Pallas kernels, per_device(): pl.pallas_call(kernel, out_shape=tuple((v(r.shape, r.dtype) for r in resu...  65.9 us

profile of v4, /device:TPU:2, one launch (start us, length us, event | category | flops | bytes accessed | tf_op | source)
XLA Modules:
  0.0 67.8 jit_solution(5080978734185403343)
XLA Ops:
  0.6 65.9 %shard_map.129 = (f32[64,2560]{1,0:T(8,128)S(1)}, f32[128,1280]{1,0:T(8,128)S(1)}, f32[128,1280]{1,0:T(8,128)S(1)}, f32[1,4]{1,0:T(1,128)S(1)}) custom-call(bf16[256,2560]{1,0:T(8,128)(2,1)} %bitcast.11, bf16[16,2560]{1,0:T(8,128)(2,1)} %bitcast.12, s32[32,256]{1,0:T(8,128)} %slots_ref.1, s32[1,256]{1,0:T(1,128)} %seg_ref.1, s32[1,4]{1,0:T(1,128)} %lens_ref.1, ...), custom_call_target="tpu_custom_call" | custom-call | tf_op jit(solution)/shard_map/pallas_call | solution.py:458
  66.5 1.3 %shard_map.130 = (f32[64,2560]{1,0:T(8,128)}, f32[128,1280]{1,0:T(8,128)}, f32[128,1280]{1,0:T(8,128)}, f32[1,4]{1,0:T(1,128)}) custom-call(f32[64,2560]{1,0:T(8,128)S(1)} %get-tuple-element.12.refs_0_, f32[128,1280]{1,0:T(8,128)S(1)} %get-tuple-element.13.refs_1_, f32[128,1280]{1,0:T(8,128)S(1)} %get-tuple-element.14.refs_2_, ...), custom_call_target="tpu_custom_call" | custom-call | tf_op jit(solution)/shard_map/pallas_call | solution.py:489
